TPU v7x, 256 devices: a whole 4x4x8 slice. The times are simulated.
256 devices in a mesh: dp: 32 (over z, y), seq: 8 (over x, core).
Axes of the slice: x: 4, y: 4, z: 8, core: 2. Of those that a mesh axis runs over, the one named last changes fastest.
Arguments:
- latent_codes: bfloat16 [32, 8, 20, 256], P('dp', 'seq'), may hold values from -4 to 4
- latent_scales: bfloat16 [32, 8, 20, 64], P('dp', 'seq'), may hold values from 0.099609375 to 2
- send_list: int32 [32, 8, 32], P('dp', 'seq'), may hold values from -1 to 19, as said below
- embed_weight: bfloat16 [64, 3072], replicated, may hold values from -0.75 to 0.75
- modulation_offset: float32 [32, 3072], P('dp'), may hold values from -3 to 3
- mod_scale: float32 [32, 3072], P('dp'), may hold values from -0.9 to 0.9
- qkv_weight: bfloat16 [3072, 6144], P('dp', 'seq'), may hold values from -0.109375 to 0.109375
- text_qkv: bfloat16 [32, 128, 6144], P('dp', 'seq'), may hold values from -8 to 8
- text_len: int32 [32], P('dp'), may hold values from 32 to 128, as said below
- out_grad_img: bfloat16 [32, 1024, 2048], P('dp', 'seq'), may hold values from -6 to 6
- out_grad_txt: bfloat16 [32, 128, 2048], P('dp', 'seq'), may hold values from -6 to 6
Outputs:
- img_attn: bfloat16 [32, 1024, 2048], P('dp', 'seq')
- txt_attn: bfloat16 [32, 128, 2048], P('dp', 'seq')
- code_grad: float32 [32, 8, 20, 256], P('dp', 'seq')
- embed_grad: float32 [64, 3072], replicated
Inputs may be any that keep to these rules, and one draw needn't show every extreme that they name: `send_list`: -1 means no block; on each device every one of its 20 blocks goes to exactly one destination sample, so a device sends at most one block to each sample. `text_len`: some sample has all 128 text tokens valid.
All inputs are finite; a program needn't handle non-finite values.
Results may differ from a plain program's by a relative error of at most 0.025.
Values may be sent and summed in bfloat16 or wider, within the bound.
A program may use at most 128 MiB of HBM per device.

v0:
```python
import jax
import jax.numpy as jnp
from jax import lax
from jax.sharding import PartitionSpec as P

HD = 128


eps = 1e-06


def layer_normalize(x):
    row_average = jnp.mean(x, axis=-1, keepdims=True)
    centred = x - row_average
    inverse_deviation = lax.rsqrt(jnp.mean(centred * centred, axis=-1, keepdims=True) + eps)
    return (centred * inverse_deviation, inverse_deviation)


def norm_backward_rule(upstream_gradient, centred_normalized, inverse_deviation, scale_factor):
    gradient_values = upstream_gradient * (1.0 + scale_factor)
    gradient_average = jnp.mean(gradient_values, axis=-1, keepdims=True)
    gradient_input_average = jnp.mean(gradient_values * centred_normalized, axis=-1, keepdims=True)
    return inverse_deviation * (
        gradient_values - gradient_average - centred_normalized * gradient_input_average
    )


def attend(query, keys, values, dout, key_ok, query_ok):
    factor = 1.0 / jnp.sqrt(jnp.float32(query.shape[-1]))
    score = jnp.einsum("qhd,khd->hqk", query, keys, preferred_element_type=jnp.float32) * factor
    score = jnp.where(key_ok[None, None, :], score, jnp.float32(-1e30))
    top = jnp.max(score, axis=-1, keepdims=True)
    expo = jnp.where(key_ok[None, None, :], jnp.exp(score - top), jnp.float32(0.0))
    prob = (expo / jnp.sum(expo, axis=-1, keepdims=True)).astype(jnp.bfloat16)
    out = jnp.einsum("hqk,khd->qhd", prob, values, preferred_element_type=jnp.float32)
    out = jnp.where(query_ok[:, None, None], out, jnp.float32(0.0)).astype(jnp.bfloat16)
    dmask = jnp.where(query_ok[:, None, None], dout, jnp.zeros_like(dout))
    delta = jnp.transpose(
        jnp.sum(dmask.astype(jnp.float32) * out.astype(jnp.float32), axis=-1), (1, 0)
    )
    dprob = jnp.einsum("qhd,khd->hqk", dmask, values, preferred_element_type=jnp.float32)
    dscore = (prob.astype(jnp.float32) * (dprob - delta[:, :, None])).astype(jnp.bfloat16)
    dquery = (
        jnp.einsum("hqk,khd->qhd", dscore, keys, preferred_element_type=jnp.float32) * factor
    ).astype(jnp.bfloat16)
    dkey = (
        jnp.einsum("hqk,qhd->khd", dscore, query, preferred_element_type=jnp.float32) * factor
    ).astype(jnp.bfloat16)
    dvalue = jnp.einsum("hqk,qhd->khd", prob, dmask, preferred_element_type=jnp.float32).astype(
        jnp.bfloat16
    )
    return (out, dquery, dkey, dvalue)


def per_device(
    latent_codes,
    latent_scales,
    send_list,
    embed_weight,
    modulation_offset,
    mod_scale,
    qkv_weight,
    text_qkv,
    text_len,
    out_grad_img,
    out_grad_txt,
):
    peers = lax.axis_size("dp")
    codes = latent_codes[0, 0]
    scales = latent_scales[0, 0]
    slots = send_list[0, 0]
    channels = scales.shape[1]
    block_len = codes.shape[1] // channels
    local_count = codes.shape[0]
    used = slots >= 0
    pick = jnp.maximum(slots, 0)
    out_codes = jnp.where(used[:, None], jnp.take(codes, pick, axis=0), jnp.zeros((), jnp.bfloat16))
    out_scales = jnp.where(
        used[:, None], jnp.take(scales, pick, axis=0), jnp.zeros((), jnp.bfloat16)
    )
    got_codes, got_scales = (
        lax.all_to_all(out_codes, "dp", split_axis=0, concat_axis=0, tiled=True),
        lax.all_to_all(out_scales, "dp", split_axis=0, concat_axis=0, tiled=True),
    )
    got_f = got_scales.astype(jnp.float32)
    deq = (
        (got_codes.astype(jnp.float32).reshape(peers, block_len, channels) * got_f[:, None, :])
        .astype(jnp.bfloat16)
        .reshape(peers, block_len * channels)
    )
    live = (jnp.sum(got_f, axis=1) > 0).astype(jnp.bfloat16)
    shift_offset = modulation_offset[0]
    scale_factor = mod_scale[0]
    tokens = deq.reshape(-1, channels)
    input_values = jnp.dot(tokens, embed_weight, preferred_element_type=jnp.float32)
    centred_normalized, inverse_deviation = layer_normalize(input_values)
    normalized_local_rows, centred_normalized, inverse_deviation = (
        (centred_normalized * (1.0 + scale_factor) + shift_offset).astype(jnp.bfloat16),
        centred_normalized,
        inverse_deviation,
    )
    normed_all, live_all = (
        lax.all_gather(normalized_local_rows, "seq", axis=0, tiled=True),
        lax.all_gather(live, "seq", axis=0, tiled=True),
    )
    image_count = normed_all.shape[0]
    qkv_width = qkv_weight.shape[1]
    qkv_img = jnp.dot(
        normed_all,
        lax.all_gather(qkv_weight, "dp", axis=0, tiled=True),
        preferred_element_type=jnp.float32,
    ).astype(jnp.bfloat16)
    text_heads, grad_img, grad_txt = (
        lax.all_to_all(text_qkv[0], "seq", split_axis=1, concat_axis=0, tiled=True),
        lax.all_to_all(out_grad_img[0], "seq", split_axis=1, concat_axis=0, tiled=True),
        lax.all_to_all(out_grad_txt[0], "seq", split_axis=1, concat_axis=0, tiled=True),
    )
    heads_dev = qkv_width // (3 * HD)
    text_count = text_heads.shape[0]
    total = text_count + image_count
    joint = jnp.concatenate([text_heads, qkv_img], axis=0).reshape(total, heads_dev, 3, HD)
    text_ok = jnp.arange(text_count) < text_len[0]
    img_ok = jnp.repeat(live_all > 0, block_len)
    valid = jnp.concatenate([text_ok, img_ok])
    dout = jnp.concatenate([grad_txt, grad_img], axis=0).reshape(total, heads_dev, HD)
    out, dquery, dkey, dvalue = attend(
        joint[:, :, 0], joint[:, :, 1], joint[:, :, 2], dout, valid, valid
    )
    flat = out.reshape(total, heads_dev * HD)
    res_img, res_txt = (
        lax.all_to_all(flat[text_count:], "seq", split_axis=0, concat_axis=1, tiled=True),
        lax.all_to_all(flat[:text_count], "seq", split_axis=0, concat_axis=1, tiled=True),
    )
    dimg = jnp.stack([dquery, dkey, dvalue], axis=2)[text_count:].reshape(image_count, qkv_width)
    dnormed_part = jnp.dot(
        dimg,
        lax.all_gather(qkv_weight, "dp", axis=0, tiled=True).T,
        preferred_element_type=jnp.float32,
    )
    normalized_gradient = lax.psum_scatter(
        dnormed_part.astype(jnp.bfloat16), "seq", scatter_dimension=0, tiled=True
    ).astype(jnp.float32)
    input_gradient_narrow = norm_backward_rule(
        normalized_gradient, centred_normalized, inverse_deviation, scale_factor
    ).astype(jnp.bfloat16)
    ddeq = jnp.dot(input_gradient_narrow, embed_weight.T, preferred_element_type=jnp.float32)
    dweight = jnp.dot(
        deq.reshape(-1, channels).T, input_gradient_narrow, preferred_element_type=jnp.float32
    )
    embed_grad = lax.psum(dweight, ("dp", "seq"))
    returned = lax.all_to_all(
        ddeq.reshape(peers, block_len * channels).astype(jnp.bfloat16),
        "dp",
        split_axis=0,
        concat_axis=0,
        tiled=True,
    ).astype(jnp.float32)
    onehot = (slots[None, :] == jnp.arange(local_count)[:, None]).astype(jnp.float32)
    summed = jnp.dot(onehot, returned, precision=lax.Precision.HIGHEST)
    code_grad = (
        summed.reshape(local_count, block_len, channels) * scales.astype(jnp.float32)[:, None, :]
    ).reshape(local_count, block_len * channels)
    return (res_img[None], res_txt[None], code_grad[None, None], embed_grad)


def solution(mesh):
    return jax.shard_map(
        per_device,
        mesh=mesh,
        in_specs=(
            P("dp", "seq", None, None),
            P("dp", "seq", None, None),
            P("dp", "seq", None),
            P(),
            P("dp", None),
            P("dp", None),
            P("dp", "seq"),
            P("dp", "seq", None),
            P("dp"),
            P("dp", "seq", None),
            P("dp", "seq", None),
        ),
        out_specs=(P("dp", "seq", None), P("dp", "seq", None), P("dp", "seq", None, None), P()),
        check_vma=False,
    )
```

profile of v0, /device:TPU:1, one launch (start us, length us, event | category | flops | bytes accessed | tf_op | source)
XLA Modules:
  0.0 506.2 jit_solution(13209143617593029536)
XLA Ops:
  11.2 12.0 %all-to-all-start = ((bf16[32,1,64]{2,1,0:T(2,128)(2,1)}), bf16[32,1,64]{2,1,0:T(2,128)(2,1)S(1)}, u32[]{:S(2)}, u32[]{:S(2)}) async-start(bf16[32,1,64]{2,1,0:T(2,128)(2,1)} %copy.74), calls=%async_computation | async-start | bytes 32768 | tf_op jit(solution)/shard_map/all_to_all | solution.py:83
  26.5 5.3 %all-to-all-done = bf16[32,1,64]{2,1,0:T(2,128)(2,1)S(1)} async-done(((bf16[32,1,64]{2,1,0:T(2,128)(2,1)}), bf16[32,1,64]{2,1,0:T(2,128)(2,1)S(1)}, u32[]{:S(2)}, u32[]{:S(2)}) %all-to-all-start) | async-done | bytes 4128 | tf_op jit(solution)/shard_map/all_to_all | solution.py:83
  31.8 3.9 all-to-all-start.2
  36.5 7.7 %all-to-all-done.2 = bf16[32,2,128]{2,1,0:T(2,128)(2,1)S(1)} async-done(((bf16[32,2,128]{2,1,0:T(2,128)(2,1)}), bf16[32,2,128]{2,1,0:T(2,128)(2,1)S(1)}, u32[]{:S(2)}, u32[]{:S(2)}) %all-to-all-start.2) | async-done | bytes 16416 | tf_op jit(solution)/shard_map/all_to_all | solution.py:82
  47.8 7.5 %all-to-all-start.5 = ((bf16[16,8,256]{2,0,1:T(8,128)(2,1)}), bf16[16,8,256]{2,0,1:T(8,128)(2,1)S(1)}, u32[]{:S(2)}, u32[]{:S(2)}) async-start(bf16[16,8,256]{2,0,1:T(8,128)(2,1)} %copy.84), calls=%async_computation.5 | async-start | bytes 131072 | tf_op jit(solution)/shard_map/all_to_all | solution.py:116
  60.2 4.1 all-to-all-start.1
  64.5 5.6 %all-to-all-done.1 = bf16[16,8,768]{2,0,1:T(8,128)(2,1)S(1)} async-done(((bf16[16,8,768]{2,0,1:T(8,128)(2,1)}), bf16[16,8,768]{2,0,1:T(8,128)(2,1)S(1)}, u32[]{:S(2)}, u32[]{:S(2)}) %all-to-all-start.1) | async-done | bytes 196640 | tf_op jit(solution)/shard_map/all_to_all | solution.py:114
  70.2 4.3 all-to-all-start.6
  74.7 14.1 %all-reduce = bf16[256]{0:T(256)(128)(2,1)S(1)} all-reduce(bf16[256]{0:T(256)(128)(2,1)S(1)} %dynamic-update-slice), channel_id=1, replica_groups=mesh['dp'=32,'seq'=8] {'seq'}, use_global_device_ids=true, to_apply=%add | all-reduce | flops 256 | bytes 1024
  92.1 3.1 all-gather.5.cloned.1.call-done
  95.2 46.3 %all-gather.3.cloned.1.call-done = bf16[1024,3072]{1,0:T(8,128)(2,1)} async-done(((bf16[128,3072]{1,0:T(8,128)(2,1)}), bf16[1024,3072]{1,0:T(8,128)(2,1)}) %all-gather.3.cloned.1.call-update) | async-done | bytes 6291472 | tf_op jit(solution)/shard_map/all_gather | solution.py:103
  141.5 9.5 %convolution_convert_fusion.2 = bf16[1024,768]{0,1:T(8,128)(2,1)} fusion(bf16[1024,3072]{1,0:T(8,128)(2,1)} %all-gather.3.cloned.1.call-done, bf16[3072,768]{1,0:T(8,128)(2,1)} %all-gather.5.cloned.1.call-done), kind=kOutput, calls=%fused_computation.26 | convolution fusion | flops 4832624640 | bytes 12582912 | tf_op jit(solution)/shard_map/dot_general | solution.py:108
  154.6 10.1 %fusion.40 = (f32[2,1152]{1,0:T(2,128)}, f32[2,1152,1152]{1,2,0:T(8,128)}) fusion(bf16[1152,2,128]{2,0,1:T(8,128)(2,1)} %fusion.19, pred[1152]{0:T(1024)(128)(4,1)S(1)} %pad_add_fusion, bf16[1024,2,3,128]{3,0,1,2:T(8,128)(2,1)S(1)} %copy.78, bf16[128,2,3,128]{3,0,1,2:T(8,128)(2,1)} %copy.77), kind=kOutput, calls=%fused_computation.82 | convolution fusion | flops 693929088 | bytes 12989440 | tf_op jit(solution)/shard_map/sub | solution.py:33
  164.8 4.9 divide_convert_fusion
  171.7 1.9 fusion.6
  178.7 7.1 %convolution_convert_fusion = bf16[1024,3072]{1,0:T(8,128)(2,1)} fusion(bf16[1024,768]{0,1:T(8,128)(2,1)S(1)} %bitcast.107, bf16[3072,768]{1,0:T(8,128)(2,1)S(1)} %bitcast.128), kind=kOutput, calls=%fused_computation.12 | convolution fusion | flops 4834983936 | bytes 12582912 | tf_op jit(solution)/shard_map/dot_general | solution.py:135
  188.7 3.5 all-to-all-start.4
  192.2 37.9 %reduce-scatter.2.cloned.1.call-done = bf16[128,3072]{1,0:T(8,128)(2,1)} async-done(((bf16[1024,3072]{1,0:T(8,128)(2,1)}), bf16[128,3072]{1,0:T(8,128)(2,1)}) %reduce-scatter.2.cloned.1.call-update) | async-done | bytes 786448 | tf_op jit(solution)/shard_map/reduce_scatter | solution.py:140
  232.4 4.6 all-to-all-start.3
  240.2 6.3 %all-to-all-done.3 = bf16[8,128,256]{1,2,0:T(8,128)(2,1)S(1)} async-done(((bf16[8,128,256]{1,2,0:T(8,128)(2,1)}), bf16[8,128,256]{1,2,0:T(8,128)(2,1)S(1)}, u32[]{:S(2)}, u32[]{:S(2)}) %all-to-all-start.3) | async-done | bytes 524320 | tf_op jit(solution)/shard_map/all_to_all | solution.py:131
  246.5 9.6 %all-to-all-start.7 = ((bf16[32,2,128]{2,1,0:T(2,128)(2,1)}), bf16[32,2,128]{2,1,0:T(2,128)(2,1)S(1)}, u32[]{:S(2)}, u32[]{:S(2)}) async-start(bf16[32,2,128]{2,1,0:T(2,128)(2,1)} %reshape.248), calls=%async_computation.8 | async-start | bytes 32768 | tf_op jit(solution)/shard_map/all_to_all | solution.py:151
  257.8 6.8 %all-to-all-done.7 = bf16[32,2,128]{2,1,0:T(2,128)(2,1)S(1)} async-done(((bf16[32,2,128]{2,1,0:T(2,128)(2,1)}), bf16[32,2,128]{2,1,0:T(2,128)(2,1)S(1)}, u32[]{:S(2)}, u32[]{:S(2)}) %all-to-all-start.7) | async-done | bytes 16416 | tf_op jit(solution)/shard_map/all_to_all | solution.py:151
  265.6 232.0 %all-reduce.3.cloned.1.call-done = f32[64,3072]{1,0:T(8,128)} async-done(((f32[64,3072]{1,0:T(8,128)}), f32[64,3072]{1,0:T(8,128)}) %all-reduce.3.cloned.1.call-update) | async-done | bytes 786448 | tf_op jit(solution)/shard_map/psum | solution.py:150
  497.6 2.1 copy.123
  (135 shorter events, 40.2 us)
Async XLA Ops:
  7.2 37.9 %copy-start = (bf16[64,3072]{1,0:T(8,128)(2,1)S(1)}, bf16[64,3072]{1,0:T(8,128)(2,1)}, u32[]{:S(2)}) copy-start(bf16[64,3072]{1,0:T(8,128)(2,1)} %param.14) | copy-start | bytes 1179652
  7.2 88.0 %all-gather.5.cloned.1.call-start = ((), (), s32[]{:S(2)}) async-start(), calls=%async_computation.10 | async-start | bytes 4866048 | tf_op jit(solution)/shard_map/all_gather | solution.py:110
  11.2 20.6 %all-to-all-start = ((bf16[32,1,64]{2,1,0:T(2,128)(2,1)}), bf16[32,1,64]{2,1,0:T(2,128)(2,1)S(1)}, u32[]{:S(2)}, u32[]{:S(2)}) async-start(bf16[32,1,64]{2,1,0:T(2,128)(2,1)} %copy.74), calls=%async_computation | async-start | bytes 32768 | tf_op jit(solution)/shard_map/all_to_all | solution.py:83
  31.8 12.4 %all-to-all-start.2 = ((bf16[32,2,128]{2,1,0:T(2,128)(2,1)}), bf16[32,2,128]{2,1,0:T(2,128)(2,1)S(1)}, u32[]{:S(2)}, u32[]{:S(2)}) async-start(bf16[32,2,128]{2,1,0:T(2,128)(2,1)} %reshape.246), calls=%async_computation.2 | async-start | bytes 32768 | tf_op jit(solution)/shard_map/all_to_all | solution.py:82
  35.7 105.8 %all-gather.3.cloned.1.call-start = ((), (), s32[]{:S(2)}) async-start(), calls=%async_computation.9 | async-start | bytes 7077888 | tf_op jit(solution)/shard_map/all_gather | solution.py:103
  45.8 9.5 %copy-start.12 = (bf16[1,16,6144]{2,1,0:T(8,128)(2,1)S(1)}, bf16[1,16,6144]{2,1,0:T(8,128)(2,1)}, u32[]{:S(2)}) copy-start(bf16[1,16,6144]{2,1,0:T(8,128)(2,1)} %param.18) | copy-start | bytes 589828
  47.0 9.7 %copy-start.9 = (bf16[1,128,2048]{2,1,0:T(8,128)(2,1)S(1)}, bf16[1,128,2048]{2,1,0:T(8,128)(2,1)}, u32[]{:S(2)}) copy-start(bf16[1,128,2048]{2,1,0:T(8,128)(2,1)} %param.20) | copy-start | bytes 1572868
  47.0 10.7 %copy-start.20 = (u32[256]{0:T(256)S(1)}, u32[256]{0:T(256)}, u32[]{:S(2)}) copy-start(u32[256]{0:T(256)} %constant.65) | copy-start | bytes 3076
  47.8 12.4 %all-to-all-start.5 = ((bf16[16,8,256]{2,0,1:T(8,128)(2,1)}), bf16[16,8,256]{2,0,1:T(8,128)(2,1)S(1)}, u32[]{:S(2)}, u32[]{:S(2)}) async-start(bf16[16,8,256]{2,0,1:T(8,128)(2,1)} %copy.84), calls=%async_computation.5 | async-start | bytes 131072 | tf_op jit(solution)/shard_map/all_to_all | solution.py:116
  60.2 10.0 %all-to-all-start.1 = ((bf16[16,8,768]{2,0,1:T(8,128)(2,1)}), bf16[16,8,768]{2,0,1:T(8,128)(2,1)S(1)}, u32[]{:S(2)}, u32[]{:S(2)}) async-start(bf16[16,8,768]{2,0,1:T(8,128)(2,1)} %copy.75), calls=%async_computation.1 | async-start | bytes 393216 | tf_op jit(solution)/shard_map/all_to_all | solution.py:114
  70.2 20.6 %all-to-all-start.6 = ((bf16[128,8,256]{0,2,1:T(8,128)(2,1)}), bf16[128,8,256]{0,2,1:T(8,128)(2,1)S(1)}, u32[]{:S(2)}, u32[]{:S(2)}) async-start(bf16[128,8,256]{0,2,1:T(8,128)(2,1)} %bitcast.23), calls=%async_computation.6 | async-start | bytes 1048576 | tf_op jit(solution)/shard_map/all_to_all | solution.py:115
  74.5 155.6 %reduce-scatter.2.cloned.1.call-start = ((), (), s32[]{:S(2)}) async-start(), calls=%async_computation.11 | async-start | bytes 7077888 | tf_op jit(solution)/shard_map/reduce_scatter | solution.py:140
  164.8 4.9 copy-start.2
  164.8 4.9 copy-start.5
  164.8 5.0 copy-start.7
  186.8 43.2 %copy-start.16 = (f32[128]{0:T(128)S(1)}, f32[128]{0:T(128)}, u32[]{:S(2)}) copy-start(f32[128]{0:T(128)} %copy-done.15) | copy-start | bytes 1540
  186.9 43.2 %copy-start.18 = (f32[128]{0:T(128)S(1)}, f32[128]{0:T(128)}, u32[]{:S(2)}) copy-start(f32[128]{0:T(128)} %copy-done.17) | copy-start | bytes 1540
  188.7 43.7 %all-to-all-start.4 = ((bf16[8,16,256]{2,1,0:T(8,128)(2,1)}), bf16[8,16,256]{2,1,0:T(8,128)(2,1)S(1)}, u32[]{:S(2)}, u32[]{:S(2)}) async-start(bf16[8,16,256]{2,1,0:T(8,128)(2,1)} %all_to_all.82), calls=%async_computation.4 | async-start | bytes 131072 | tf_op jit(solution)/shard_map/all_to_all | solution.py:132
  231.8 5.2 %copy-start.11 = (bf16[128,64]{1,0:T(8,128)(2,1)S(1)}, bf16[128,64]{1,0:T(8,128)(2,1)}, u32[]{:S(2)}) copy-start(bf16[128,64]{1,0:T(8,128)(2,1)} %copy-done.10) | copy-start | bytes 49156
  232.4 14.1 %all-to-all-start.3 = ((bf16[8,128,256]{1,2,0:T(8,128)(2,1)}), bf16[8,128,256]{1,2,0:T(8,128)(2,1)S(1)}, u32[]{:S(2)}, u32[]{:S(2)}) async-start(bf16[8,128,256]{1,2,0:T(8,128)(2,1)} %copy.81), calls=%async_computation.3 | async-start | bytes 1048576 | tf_op jit(solution)/shard_map/all_to_all | solution.py:131
  237.0 19.1 %copy-start.6 = (bf16[1,1,20,64]{3,2,1,0:T(8,128)(2,1)S(1)}, bf16[1,1,20,64]{3,2,1,0:T(8,128)(2,1)}, u32[]{:S(2)}) copy-start(bf16[1,1,20,64]{3,2,1,0:T(8,128)(2,1)} %param.12) | copy-start | bytes 7684
  237.0 260.6 %all-reduce.3.cloned.1.call-start = ((), (), s32[]{:S(2)}) async-start(), calls=%async_computation.12 | async-start | bytes 1572864 | tf_op jit(solution)/shard_map/psum | solution.py:150
  238.2 26.5 %copy-start.19 = (s32[1,1,32]{2,1,0:T(1,128)S(1)}, s32[1,1,32]{2,1,0:T(1,128)}, u32[]{:S(2)}) copy-start(s32[1,1,32]{2,1,0:T(1,128)} %param.13) | copy-start | bytes 388
  246.5 18.1 %all-to-all-start.7 = ((bf16[32,2,128]{2,1,0:T(2,128)(2,1)}), bf16[32,2,128]{2,1,0:T(2,128)(2,1)S(1)}, u32[]{:S(2)}, u32[]{:S(2)}) async-start(bf16[32,2,128]{2,1,0:T(2,128)(2,1)} %reshape.248), calls=%async_computation.8 | async-start | bytes 32768 | tf_op jit(solution)/shard_map/all_to_all | solution.py:151
  (11 other events, 18.2 us)
Sparse Core Ops, SparseCore 0:
  10.6 84.5 all-gather.4
  97.6 43.8 all-gather.2
  185.9 44.1 reduce-scatter.1
  243.5 253.9 all-reduce.2
where the time goes:
time: 508 us; the launch traced here: 506 us
  waiting for transfers between devices  353 us (69%)
  starting transfers between devices  49.6 us (10%)
  matrix products  37.2 us (7%)
  local copies, waits for them, and re-layouts  22 us (4%)
  between operations  15.5 us (3%)
  other arithmetic  14.7 us (3%)
  blocking collectives  14.1 us (3%)
    psum x1, waiting for transfers between devices, per_device(): embed_grad = lax.psum(dweight, ('dp', 'seq'))  232 us
    all_gather x1, waiting for transfers between devices, per_device(): lax.all_gather(normalized_local_rows, 'seq', axis=0, tiled=True)  46.3 us
    reduce_scatter x1, waiting for transfers between devices, per_device(): lax.psum_scatter(dnormed_part.astype(jnp.bfloat16), 'seq', scatter_dimens...  37.9 us
    unnamed x1, blocking collectives  14.1 us
    all_to_all x1, starting transfers between devices, per_device(): lax.all_to_all(out_scales, 'dp', split_axis=0, concat_axis=0, tiled=True)  12 us
  transfers between devices with their start and end apart: 12, of which 10 were waited for; matrix products, arithmetic and copies ran while one was open for 5% of the time, Pallas kernels for 0%

commit v1 on v0

--- a/solution.py
+++ b/solution.py
@@ -14,15 +14,6 @@
     centred = x - row_average
     inverse_deviation = lax.rsqrt(jnp.mean(centred * centred, axis=-1, keepdims=True) + eps)
     return (centred * inverse_deviation, inverse_deviation)
-
-
-def norm_backward_rule(upstream_gradient, centred_normalized, inverse_deviation, scale_factor):
-    gradient_values = upstream_gradient * (1.0 + scale_factor)
-    gradient_average = jnp.mean(gradient_values, axis=-1, keepdims=True)
-    gradient_input_average = jnp.mean(gradient_values * centred_normalized, axis=-1, keepdims=True)
-    return inverse_deviation * (
-        gradient_values - gradient_average - centred_normalized * gradient_input_average
-    )
 
 
 def attend(query, keys, values, dout, key_ok, query_ok):
@@ -50,6 +41,12 @@
         jnp.bfloat16
     )
     return (out, dquery, dkey, dvalue)
+
+
+def split2(value):
+    high = value.astype(jnp.bfloat16)
+    low = (value - high.astype(jnp.float32)).astype(jnp.bfloat16)
+    return jnp.concatenate([high, low], axis=0)
 
 
 def per_device(
@@ -92,23 +89,33 @@
     shift_offset = modulation_offset[0]
     scale_factor = mod_scale[0]
     tokens = deq.reshape(-1, channels)
+    width = embed_weight.shape[1]
     input_values = jnp.dot(tokens, embed_weight, preferred_element_type=jnp.float32)
     centred_normalized, inverse_deviation = layer_normalize(input_values)
-    normalized_local_rows, centred_normalized, inverse_deviation = (
-        (centred_normalized * (1.0 + scale_factor) + shift_offset).astype(jnp.bfloat16),
-        centred_normalized,
-        inverse_deviation,
-    )
-    normed_all, live_all = (
-        lax.all_gather(normalized_local_rows, "seq", axis=0, tiled=True),
-        lax.all_gather(live, "seq", axis=0, tiled=True),
-    )
-    image_count = normed_all.shape[0]
+    embed_f = embed_weight.astype(jnp.float32)
+    embed_centred = embed_f - jnp.mean(embed_f, axis=1, keepdims=True)
+    packed = jnp.concatenate(
+        [tokens.astype(jnp.float32), inverse_deviation, jnp.repeat(live, block_len)[:, None].astype(jnp.float32)],
+        axis=1,
+    )
+    packed_all = lax.all_gather(packed, "seq", axis=0, tiled=True)
+    tokens_all = packed_all[:, :channels].astype(jnp.bfloat16)
+    inv_all = packed_all[:, channels : channels + 1]
+    live_all = packed_all[:, channels + 1]
+    image_count = packed_all.shape[0]
     qkv_width = qkv_weight.shape[1]
-    qkv_img = jnp.dot(
-        normed_all,
-        lax.all_gather(qkv_weight, "dp", axis=0, tiled=True),
-        preferred_element_type=jnp.float32,
+    weight = lax.all_gather(qkv_weight, "dp", axis=0, tiled=True)
+    modulated = split2(jnp.concatenate([embed_centred * (1.0 + scale_factor), shift_offset[None]], axis=0))
+    product = jnp.dot(modulated, weight, preferred_element_type=jnp.float32)
+    product = product[: channels + 1] + product[channels + 1 :]
+    mixed, constant = product[:channels], product[channels:]
+    mixed2 = split2(mixed)
+    qkv_img = (
+        jnp.dot(
+            jnp.concatenate([tokens_all, tokens_all], axis=1), mixed2, preferred_element_type=jnp.float32
+        )
+        * inv_all
+        + constant
     ).astype(jnp.bfloat16)
     text_heads, grad_img, grad_txt = (
         lax.all_to_all(text_qkv[0], "seq", split_axis=1, concat_axis=0, tiled=True),
@@ -120,7 +127,7 @@
     total = text_count + image_count
     joint = jnp.concatenate([text_heads, qkv_img], axis=0).reshape(total, heads_dev, 3, HD)
     text_ok = jnp.arange(text_count) < text_len[0]
-    img_ok = jnp.repeat(live_all > 0, block_len)
+    img_ok = live_all > 0
     valid = jnp.concatenate([text_ok, img_ok])
     dout = jnp.concatenate([grad_txt, grad_img], axis=0).reshape(total, heads_dev, HD)
     out, dquery, dkey, dvalue = attend(
@@ -132,22 +139,52 @@
         lax.all_to_all(flat[:text_count], "seq", split_axis=0, concat_axis=1, tiled=True),
     )
     dimg = jnp.stack([dquery, dkey, dvalue], axis=2)[text_count:].reshape(image_count, qkv_width)
-    dnormed_part = jnp.dot(
-        dimg,
-        lax.all_gather(qkv_weight, "dp", axis=0, tiled=True).T,
+    grad_part = lax.dot_general(
+        dimg, mixed2[:channels], (((1,), (1,)), ((), ())), preferred_element_type=jnp.float32
+    )
+    scaled = tokens_all.astype(jnp.float32) * inv_all
+    project = jnp.sum(scaled * grad_part, axis=1, keepdims=True) * (1.0 / width)
+    gram = lax.dot_general(
+        (scaled * inv_all * project).astype(jnp.bfloat16),
+        tokens_all,
+        (((0,), (0,)), ((), ())),
         preferred_element_type=jnp.float32,
     )
-    normalized_gradient = lax.psum_scatter(
-        dnormed_part.astype(jnp.bfloat16), "seq", scatter_dimension=0, tiled=True
-    ).astype(jnp.float32)
-    input_gradient_narrow = norm_backward_rule(
-        normalized_gradient, centred_normalized, inverse_deviation, scale_factor
-    ).astype(jnp.bfloat16)
-    ddeq = jnp.dot(input_gradient_narrow, embed_weight.T, preferred_element_type=jnp.float32)
-    dweight = jnp.dot(
-        deq.reshape(-1, channels).T, input_gradient_narrow, preferred_element_type=jnp.float32
-    )
-    embed_grad = lax.psum(dweight, ("dp", "seq"))
+    seen = lax.dot_general(
+        scaled.astype(jnp.bfloat16), dimg, (((0,), (0,)), ((), ())), preferred_element_type=jnp.float32
+    ).astype(jnp.bfloat16)
+    dweight = lax.dot_general(
+        seen, weight, (((1,), (1,)), ((), ())), preferred_element_type=jnp.float32
+    ) * (1.0 + scale_factor)
+    dweight = dweight - jnp.mean(dweight, axis=1, keepdims=True)
+    dweight = dweight - jnp.dot(gram.astype(jnp.bfloat16), embed_centred.astype(jnp.bfloat16), preferred_element_type=jnp.float32)
+    members = lax.axis_size("seq")
+    part = lax.all_to_all(
+        dweight.reshape(channels, members, width // members).astype(jnp.bfloat16), "seq", split_axis=1, concat_axis=1, tiled=True
+    )
+    part = jnp.sum(part.astype(jnp.float32), axis=1)
+    part = lax.all_to_all(
+        part.reshape(peers, -1), "dp", split_axis=0, concat_axis=0, tiled=True
+    )
+    part = jnp.sum(part, axis=0)
+    part = lax.all_gather(part, "dp", axis=0, tiled=True).reshape(channels, width // members)
+    embed_grad = lax.all_gather(part, "seq", axis=1, tiled=True)
+    grad_own = jnp.sum(
+        lax.all_to_all(
+            grad_part.reshape(members, -1, channels).astype(jnp.bfloat16), "seq", split_axis=0, concat_axis=0, tiled=True
+        ).astype(jnp.float32),
+        axis=0,
+    )
+    project_own = (
+        jnp.sum(tokens.astype(jnp.float32) * grad_own, axis=1, keepdims=True) * inverse_deviation * (1.0 / width)
+    )
+    back = lax.dot_general(
+        centred_normalized.astype(jnp.bfloat16),
+        embed_weight,
+        (((1,), (1,)), ((), ())),
+        preferred_element_type=jnp.float32,
+    )
+    ddeq = inverse_deviation * (grad_own - back * project_own)
     returned = lax.all_to_all(
         ddeq.reshape(peers, block_len * channels).astype(jnp.bfloat16),
         "dp",

time: 508 us -> 280 us (0.55)
  waiting for transfers between devices: 353 us -> 47.7 us
  blocking collectives: 14.1 us -> 73.7 us
  starting transfers between devices: 49.6 us -> 65.8 us
  matrix products: 37.2 us -> 32 us
    psum x1 -> x0, waiting for transfers between devices: 232 us -> none  [per_device(): embed_grad = lax.psum(dweight, ('dp', 'seq'))]
    all_gather x0 -> x3, blocking collectives: none -> 73.7 us  [the longest x1 31.1 us: per_device(): lax.all_gather(part, 'dp', axis=0, tiled=True)]
    all_gather x2 -> x1, waiting for transfers between devices: 49.4 us -> 0.01 us  [per_device(): weight = lax.all_gather(qkv_weight, 'dp', axis=0, tiled=True)]
    reduce_scatter x1 -> x0, waiting for transfers between devices: 37.9 us -> none  [per_device(): lax.psum_scatter(dnormed_part.astype(jnp.bfloat16), 'seq', scatter_dimens...]
    all_to_all x0 -> x3, starting transfers between devices: none -> 15 us  [the longest x1 6.23 us: per_device(): lax.all_to_all(dweight.reshape(channels, members, width // members).astyp...]
    all_to_all x0 -> x3, waiting for transfers between devices: none -> 14.2 us  [the longest x1 7.24 us: per_device(): lax.all_to_all(part.reshape(peers, -1), 'dp', split_axis=0, concat_axis=0...]
    unnamed x1 -> x0, blocking collectives: 14.1 us -> none
    all_to_all x1, waiting for transfers between devices: 5.32 us -> 0.01 us  [per_device(): lax.all_to_all(out_scales, 'dp', split_axis=0, concat_axis=0, tiled=True)]
  transfers between devices with their start and end apart: 12 -> 12, of which waited for: 10 -> 7; matrix products, arithmetic and copies ran while one was open for 5% -> 14% of each run, Pallas kernels for 0% -> 0%
where the time goes in v1:
time: 280 us; the launch traced here: 279 us
  blocking collectives  73.7 us (26%)
  starting transfers between devices  65.8 us (24%)
  waiting for transfers between devices  47.7 us (17%)
  matrix products  32 us (11%)
  local copies, waits for them, and re-layouts  25.3 us (9%)
  other arithmetic  19 us (7%)
  between operations  15.3 us (5%)
    all_gather x1, blocking collectives, per_device(): lax.all_gather(part, 'dp', axis=0, tiled=True)  31.1 us
    all_gather x1, blocking collectives, per_device(): embed_grad = lax.all_gather(part, 'seq', axis=1, tiled=True)  25.4 us
    all_gather x1, blocking collectives, per_device(): packed_all = lax.all_gather(packed, 'seq', axis=0, tiled=True)  17.1 us
    all_to_all x1, starting transfers between devices, per_device(): lax.all_to_all(out_scales, 'dp', split_axis=0, concat_axis=0, tiled=True)  12 us
    sub x1, matrix products, attend(): score - top  10.1 us
    all_to_all x1, starting transfers between devices, per_device(): lax.all_to_all(out_codes, 'dp', split_axis=0, concat_axis=0, tiled=True)  9.21 us
    all_to_all x1, waiting for transfers between devices, per_device(): lax.all_to_all(out_codes, 'dp', split_axis=0, concat_axis=0, tiled=True)  7.98 us
    all_to_all x1, waiting for transfers between devices, per_device(): lax.all_to_all(flat[text_count:], 'seq', split_axis=0, concat_axis=1, til...  7.88 us
  transfers between devices with their start and end apart: 12, of which 7 were waited for; matrix products, arithmetic and copies ran while one was open for 14% of the time, Pallas kernels for 0%

profile of v1, /device:TPU:1, one launch (start us, length us, event | category | flops | bytes accessed | tf_op | source)
XLA Modules:
  0.0 278.9 jit_solution(6379386644889509573)
XLA Ops:
  11.2 12.0 %all-to-all-start.1 = ((bf16[32,1,64]{2,1,0:T(2,128)(2,1)}), bf16[32,1,64]{2,1,0:T(2,128)(2,1)S(1)}, u32[]{:S(2)}, u32[]{:S(2)}) async-start(bf16[32,1,64]{2,1,0:T(2,128)(2,1)} %copy.80), calls=%async_computation.1 | async-start | bytes 32768 | tf_op jit(solution)/shard_map/all_to_all | solution.py:80
  32.9 9.2 %all-to-all-start = ((bf16[32,2,128]{2,1,0:T(2,128)(2,1)}), bf16[32,2,128]{2,1,0:T(2,128)(2,1)S(1)}, u32[]{:S(2)}, u32[]{:S(2)}) async-start(bf16[32,2,128]{2,1,0:T(2,128)(2,1)} %reshape.312), calls=%async_computation | async-start | bytes 32768 | tf_op jit(solution)/shard_map/all_to_all | solution.py:79
  42.7 8.0 %all-to-all-done = bf16[32,2,128]{2,1,0:T(2,128)(2,1)S(1)} async-done(((bf16[32,2,128]{2,1,0:T(2,128)(2,1)}), bf16[32,2,128]{2,1,0:T(2,128)(2,1)S(1)}, u32[]{:S(2)}, u32[]{:S(2)}) %all-to-all-start) | async-done | bytes 16416 | tf_op jit(solution)/shard_map/all_to_all | solution.py:79
  50.7 6.8 %all-to-all-start.5 = ((bf16[16,8,256]{2,0,1:T(8,128)(2,1)}), bf16[16,8,256]{2,0,1:T(8,128)(2,1)S(1)}, u32[]{:S(2)}, u32[]{:S(2)}) async-start(bf16[16,8,256]{2,0,1:T(8,128)(2,1)} %copy.91), calls=%async_computation.5 | async-start | bytes 131072 | tf_op jit(solution)/shard_map/all_to_all | solution.py:123
  58.3 4.1 %all-to-all-done.5 = bf16[16,8,256]{2,0,1:T(8,128)(2,1)S(1)} async-done(((bf16[16,8,256]{2,0,1:T(8,128)(2,1)}), bf16[16,8,256]{2,0,1:T(8,128)(2,1)S(1)}, u32[]{:S(2)}, u32[]{:S(2)}) %all-to-all-start.5) | async-done | bytes 65568 | tf_op jit(solution)/shard_map/all_to_all | solution.py:123
  62.4 4.1 %all-to-all-start.2 = ((bf16[16,8,768]{2,0,1:T(8,128)(2,1)}), bf16[16,8,768]{2,0,1:T(8,128)(2,1)S(1)}, u32[]{:S(2)}, u32[]{:S(2)}) async-start(bf16[16,8,768]{2,0,1:T(8,128)(2,1)} %copy.83), calls=%async_computation.2 | async-start | bytes 393216 | tf_op jit(solution)/shard_map/all_to_all | solution.py:121
  66.8 5.6 %all-to-all-done.2 = bf16[16,8,768]{2,0,1:T(8,128)(2,1)S(1)} async-done(((bf16[16,8,768]{2,0,1:T(8,128)(2,1)}), bf16[16,8,768]{2,0,1:T(8,128)(2,1)S(1)}, u32[]{:S(2)}, u32[]{:S(2)}) %all-to-all-start.2) | async-done | bytes 196640 | tf_op jit(solution)/shard_map/all_to_all | solution.py:121
  72.4 4.3 %all-to-all-start.6 = ((bf16[128,8,256]{0,2,1:T(8,128)(2,1)}), bf16[128,8,256]{0,2,1:T(8,128)(2,1)S(1)}, u32[]{:S(2)}, u32[]{:S(2)}) async-start(bf16[128,8,256]{0,2,1:T(8,128)(2,1)} %bitcast.23), calls=%async_computation.6 | async-start | bytes 1048576 | tf_op jit(solution)/shard_map/all_to_all | solution.py:122
  76.8 17.1 %all_gather.12 = f32[1024,66]{0,1:T(8,128)S(1)} all-gather(f32[128,66]{0,1:T(8,128)S(1)} %pad_maximum_fusion.4), channel_id=1, replica_groups=mesh['dp'=32,'seq'=8] {'seq'}, dimensions={0}, use_global_device_ids=true | all-gather | bytes 304128 | tf_op jit(solution)/shard_map/all_gather | solution.py:101
  107.1 10.1 %fusion.74 = (f32[2,1152]{1,0:T(2,128)}, f32[2,1152,1152]{1,2,0:T(8,128)}) fusion(bf16[1152,2,128]{2,0,1:T(8,128)(2,1)} %fusion.31, pred[1152]{0:T(1024)(128)(4,1)} %pad_add_fusion, bf16[1024,2,3,128]{3,0,1,2:T(8,128)(2,1)S(1)} %copy.85, bf16[128,2,3,128]{3,0,1,2:T(8,128)(2,1)} %copy.84), kind=kOutput, calls=%fused_computation.130 | convolution fusion | flops 693929088 | bytes 12989440 | tf_op jit(solution)/shard_map/sub | solution.py:24
  117.2 4.9 %divide_convert_fusion = bf16[2,1152,1152]{1,2,0:T(8,128)(2,1)S(1)} fusion(f32[2,1152,1152]{1,2,0:T(8,128)} %get-tuple-element.29, f32[2,1152]{1,0:T(2,128)} %get-tuple-element.28), kind=kLoop, calls=%fused_computation.11 | loop fusion | flops 5308416 | bytes 15934464 | tf_op jit(solution)/shard_map/convert_element_type | solution.py:25
  133.3 4.9 %all-to-all-start.7 = ((bf16[8,128,64]{1,2,0:T(8,128)(2,1)}), bf16[8,128,64]{1,2,0:T(8,128)(2,1)}, u32[]{:S(2)}, u32[]{:S(2)}) async-start(bf16[8,128,64]{1,2,0:T(8,128)(2,1)} %bitcast.123), calls=%async_computation.7 | async-start | bytes 262144 | tf_op jit(solution)/shard_map/all_to_all | solution.py:173
  142.8 6.1 %fusion.77 = (f32[64]{0:T(128)}, f32[64,3072]{1,0:T(8,128)}) fusion(f32[3072]{0:T(1024)} %bitcast.130, bf16[3072,768]{1,0:T(8,128)(2,1)} %all-gather.3.cloned.1.call-done, bf16[1024,768]{0,1:T(8,128)(2,1)S(1)} %bitcast.113, f32[1024]{0:T(1024)S(1)} %bitcast.133, f32[1024,66]{0,1:T(8,128)} %copy-done.2), kind=kOutput, calls=%fused_computation.131 | convolution fusion | flops 403292096 | bytes 7225600 | tf_op jit(solution)/shard_map/dot_general | solution.py:156
  149.6 4.8 %all-to-all-start.4 = ((bf16[8,16,256]{2,1,0:T(8,128)(2,1)}), bf16[8,16,256]{2,1,0:T(8,128)(2,1)S(1)}, u32[]{:S(2)}, u32[]{:S(2)}) async-start(bf16[8,16,256]{2,1,0:T(8,128)(2,1)} %all_to_all.94), calls=%async_computation.4 | async-start | bytes 131072 | tf_op jit(solution)/shard_map/all_to_all | solution.py:139
  159.4 5.3 %all-to-all-start.8 = ((bf16[32,2,128]{2,1,0:T(2,128)(2,1)}), bf16[32,2,128]{2,1,0:T(2,128)(2,1)S(1)}, u32[]{:S(2)}, u32[]{:S(2)}) async-start(bf16[32,2,128]{2,1,0:T(2,128)(2,1)} %reshape.314), calls=%async_computation.8 | async-start | bytes 32768 | tf_op jit(solution)/shard_map/all_to_all | solution.py:188
  166.0 7.2 %all-to-all-done.8 = bf16[32,2,128]{2,1,0:T(2,128)(2,1)S(1)} async-done(((bf16[32,2,128]{2,1,0:T(2,128)(2,1)}), bf16[32,2,128]{2,1,0:T(2,128)(2,1)S(1)}, u32[]{:S(2)}, u32[]{:S(2)}) %all-to-all-start.8) | async-done | bytes 16416 | tf_op jit(solution)/shard_map/all_to_all | solution.py:188
  173.2 6.2 %all-to-all-start.9 = ((bf16[64,8,384]{2,0,1:T(8,128)(2,1)}), bf16[64,8,384]{2,0,1:T(8,128)(2,1)S(1)}, u32[]{:S(2)}, u32[]{:S(2)}) async-start(bf16[64,8,384]{2,0,1:T(8,128)(2,1)} %bitcast.107), calls=%async_computation.9 | async-start | bytes 786432 | tf_op jit(solution)/shard_map/all_to_all | solution.py:162
  180.5 7.0 %all-to-all-done.9 = bf16[64,8,384]{2,0,1:T(8,128)(2,1)S(1)} async-done(((bf16[64,8,384]{2,0,1:T(8,128)(2,1)}), bf16[64,8,384]{2,0,1:T(8,128)(2,1)S(1)}, u32[]{:S(2)}, u32[]{:S(2)}) %all-to-all-start.9) | async-done | bytes 393248 | tf_op jit(solution)/shard_map/all_to_all | solution.py:162
  187.5 4.3 %all-to-all-start.3 = ((bf16[8,128,256]{1,2,0:T(8,128)(2,1)}), bf16[8,128,256]{1,2,0:T(8,128)(2,1)S(1)}, u32[]{:S(2)}, u32[]{:S(2)}) async-start(bf16[8,128,256]{1,2,0:T(8,128)(2,1)} %copy.88), calls=%async_computation.3 | async-start | bytes 1048576 | tf_op jit(solution)/shard_map/all_to_all | solution.py:138
  193.4 7.9 %all-to-all-done.3 = bf16[8,128,256]{1,2,0:T(8,128)(2,1)S(1)} async-done(((bf16[8,128,256]{1,2,0:T(8,128)(2,1)}), bf16[8,128,256]{1,2,0:T(8,128)(2,1)S(1)}, u32[]{:S(2)}, u32[]{:S(2)}) %all-to-all-start.3) | async-done | bytes 524320 | tf_op jit(solution)/shard_map/all_to_all | solution.py:138
  201.2 3.9 %all-to-all-start.10 = ((f32[32,1,768]{2,1,0:T(1,128)}), f32[32,1,768]{2,1,0:T(1,128)S(1)}, u32[]{:S(2)}, u32[]{:S(2)}) async-start(f32[32,1,768]{2,1,0:T(1,128)} %all_to_all.107), calls=%async_computation.10 | async-start | bytes 196608 | tf_op jit(solution)/shard_map/all_to_all | solution.py:166
  207.0 7.2 %all-to-all-done.10 = f32[32,1,768]{2,1,0:T(1,128)S(1)} async-done(((f32[32,1,768]{2,1,0:T(1,128)}), f32[32,1,768]{2,1,0:T(1,128)S(1)}, u32[]{:S(2)}, u32[]{:S(2)}) %all-to-all-start.10) | async-done | bytes 98336 | tf_op jit(solution)/shard_map/all_to_all | solution.py:166
  214.3 31.1 %all-gather = f32[32,1,768]{2,1,0:T(1,128)S(1)} all-gather(f32[1,1,768]{2,1,0:T(1,128)S(1)} %reshape.304), channel_id=1, replica_groups=mesh['dp'=32,'seq'=8] {'dp'}, dimensions={0}, use_global_device_ids=true | all-gather | bytes 101376 | tf_op jit(solution)/shard_map/all_gather | solution.py:170
  245.7 25.4 %all_gather.15 = f32[64,3072]{1,0:T(8,128)S(1)} all-gather(f32[64,384]{1,0:T(8,128)S(1)} %reshape.283), channel_id=1, replica_groups=mesh['dp'=32,'seq'=8] {'seq'}, dimensions={1}, use_global_device_ids=true | all-gather | bytes 884736 | tf_op jit(solution)/shard_map/all_gather | solution.py:171
  (166 shorter events, 56.0 us)
Async XLA Ops:
  7.2 16.1 %copy-start = (bf16[1,1,20,256]{3,2,1,0:T(8,128)(2,1)S(1)}, bf16[1,1,20,256]{3,2,1,0:T(8,128)(2,1)}, u32[]{:S(2)}) copy-start(bf16[1,1,20,256]{3,2,1,0:T(8,128)(2,1)} %param.11) | copy-start | bytes 30724
  7.2 20.5 %copy-start.22 = (f32[1,3072]{1,0:T(1,128)S(1)}, f32[1,3072]{1,0:T(1,128)}, u32[]{:S(2)}) copy-start(f32[1,3072]{1,0:T(1,128)} %param.15) | copy-start | bytes 36868
  7.2 91.1 %all-gather.3.cloned.1.call-start = ((), (), s32[]{:S(2)}) async-start(), calls=%async_computation.11 | async-start | bytes 4866048 | tf_op jit(solution)/shard_map/all_gather | solution.py:107
  11.2 21.7 %all-to-all-start.1 = ((bf16[32,1,64]{2,1,0:T(2,128)(2,1)}), bf16[32,1,64]{2,1,0:T(2,128)(2,1)S(1)}, u32[]{:S(2)}, u32[]{:S(2)}) async-start(bf16[32,1,64]{2,1,0:T(2,128)(2,1)} %copy.80), calls=%async_computation.1 | async-start | bytes 32768 | tf_op jit(solution)/shard_map/all_to_all | solution.py:80
  28.7 29.2 %copy-start.1 = (bf16[64,3072]{1,0:T(8,128)(2,1)S(1)}, bf16[64,3072]{1,0:T(8,128)(2,1)}, u32[]{:S(2)}) copy-start(bf16[64,3072]{1,0:T(8,128)(2,1)} %param.14) | copy-start | bytes 1179652
  32.9 17.8 %all-to-all-start = ((bf16[32,2,128]{2,1,0:T(2,128)(2,1)}), bf16[32,2,128]{2,1,0:T(2,128)(2,1)S(1)}, u32[]{:S(2)}, u32[]{:S(2)}) async-start(bf16[32,2,128]{2,1,0:T(2,128)(2,1)} %reshape.312), calls=%async_computation | async-start | bytes 32768 | tf_op jit(solution)/shard_map/all_to_all | solution.py:79
  50.7 11.7 %all-to-all-start.5 = ((bf16[16,8,256]{2,0,1:T(8,128)(2,1)}), bf16[16,8,256]{2,0,1:T(8,128)(2,1)S(1)}, u32[]{:S(2)}, u32[]{:S(2)}) async-start(bf16[16,8,256]{2,0,1:T(8,128)(2,1)} %copy.91), calls=%async_computation.5 | async-start | bytes 131072 | tf_op jit(solution)/shard_map/all_to_all | solution.py:123
  58.3 18.4 %copy-start.27 = (f32[128]{0:T(128)}, f32[128]{0:T(128)S(1)}, u32[]{:S(2)}) copy-start(f32[128]{0:T(128)S(1)} %broadcast_multiply_fusion.3) | copy-start | bytes 1540
  62.4 10.0 %all-to-all-start.2 = ((bf16[16,8,768]{2,0,1:T(8,128)(2,1)}), bf16[16,8,768]{2,0,1:T(8,128)(2,1)S(1)}, u32[]{:S(2)}, u32[]{:S(2)}) async-start(bf16[16,8,768]{2,0,1:T(8,128)(2,1)} %copy.83), calls=%async_computation.2 | async-start | bytes 393216 | tf_op jit(solution)/shard_map/all_to_all | solution.py:121
  66.8 10.0 %copy-start.24 = (f32[128]{0:T(128)}, f32[128]{0:T(128)S(1)}, u32[]{:S(2)}) copy-start(f32[128]{0:T(128)S(1)} %multiply_reduce_fusion) | copy-start | bytes 1540
  72.4 24.5 %all-to-all-start.6 = ((bf16[128,8,256]{0,2,1:T(8,128)(2,1)}), bf16[128,8,256]{0,2,1:T(8,128)(2,1)S(1)}, u32[]{:S(2)}, u32[]{:S(2)}) async-start(bf16[128,8,256]{0,2,1:T(8,128)(2,1)} %bitcast.23), calls=%async_computation.6 | async-start | bytes 1048576 | tf_op jit(solution)/shard_map/all_to_all | solution.py:122
  133.3 16.3 %all-to-all-start.7 = ((bf16[8,128,64]{1,2,0:T(8,128)(2,1)}), bf16[8,128,64]{1,2,0:T(8,128)(2,1)}, u32[]{:S(2)}, u32[]{:S(2)}) async-start(bf16[8,128,64]{1,2,0:T(8,128)(2,1)} %bitcast.123), calls=%async_computation.7 | async-start | bytes 262144 | tf_op jit(solution)/shard_map/all_to_all | solution.py:173
  148.9 15.8 %copy-start.4 = (f32[1024,66]{0,1:T(8,128)S(1)}, f32[1024,66]{0,1:T(8,128)}, u32[]{:S(2)}) copy-start(f32[1024,66]{0,1:T(8,128)} %copy-done.2) | copy-start | bytes 811012
  148.9 15.8 %copy-start.8 = (f32[64,3072]{1,0:T(8,128)S(1)}, f32[64,3072]{1,0:T(8,128)}, u32[]{:S(2)}) copy-start(f32[64,3072]{1,0:T(8,128)} %get-tuple-element.33) | copy-start | bytes 2359300
  148.9 15.8 %copy-start.23 = (f32[1024]{0:T(1024)S(1)}, f32[1024]{0:T(1024)}, u32[]{:S(2)}) copy-start(f32[1024]{0:T(1024)} %broadcast_multiply_fusion) | copy-start | bytes 12292
  148.9 15.8 %copy-start.26 = (f32[64]{0:T(128)S(1)}, f32[64]{0:T(128)}, u32[]{:S(2)}) copy-start(f32[64]{0:T(128)} %copy-done.25) | copy-start | bytes 772
  149.6 9.7 %all-to-all-start.4 = ((bf16[8,16,256]{2,1,0:T(8,128)(2,1)}), bf16[8,16,256]{2,1,0:T(8,128)(2,1)S(1)}, u32[]{:S(2)}, u32[]{:S(2)}) async-start(bf16[8,16,256]{2,1,0:T(8,128)(2,1)} %all_to_all.94), calls=%async_computation.4 | async-start | bytes 131072 | tf_op jit(solution)/shard_map/all_to_all | solution.py:139
  159.4 13.8 %all-to-all-start.8 = ((bf16[32,2,128]{2,1,0:T(2,128)(2,1)}), bf16[32,2,128]{2,1,0:T(2,128)(2,1)S(1)}, u32[]{:S(2)}, u32[]{:S(2)}) async-start(bf16[32,2,128]{2,1,0:T(2,128)(2,1)} %reshape.314), calls=%async_computation.8 | async-start | bytes 32768 | tf_op jit(solution)/shard_map/all_to_all | solution.py:188
  164.7 14.7 %copy-start.12 = (bf16[1152,2,128]{0,2,1:T(8,128)(2,1)S(1)}, bf16[1152,2,128]{0,2,1:T(8,128)(2,1)}, u32[]{:S(2)}) copy-start(bf16[1152,2,128]{0,2,1:T(8,128)(2,1)} %get-tuple-element.31) | copy-start | bytes 1769476
  173.2 14.3 %all-to-all-start.9 = ((bf16[64,8,384]{2,0,1:T(8,128)(2,1)}), bf16[64,8,384]{2,0,1:T(8,128)(2,1)S(1)}, u32[]{:S(2)}, u32[]{:S(2)}) async-start(bf16[64,8,384]{2,0,1:T(8,128)(2,1)} %bitcast.107), calls=%async_computation.9 | async-start | bytes 786432 | tf_op jit(solution)/shard_map/all_to_all | solution.py:162
  179.5 12.3 %copy-start.10 = (bf16[1,1,20,64]{3,2,1,0:T(8,128)(2,1)S(1)}, bf16[1,1,20,64]{3,2,1,0:T(8,128)(2,1)}, u32[]{:S(2)}) copy-start(bf16[1,1,20,64]{3,2,1,0:T(8,128)(2,1)} %param.12) | copy-start | bytes 7684
  179.6 25.5 %copy-start.28 = (s32[1,1,32]{2,1,0:T(1,128)S(1)}, s32[1,1,32]{2,1,0:T(1,128)}, u32[]{:S(2)}) copy-start(s32[1,1,32]{2,1,0:T(1,128)} %param.13) | copy-start | bytes 388
  187.5 13.8 %all-to-all-start.3 = ((bf16[8,128,256]{1,2,0:T(8,128)(2,1)}), bf16[8,128,256]{1,2,0:T(8,128)(2,1)S(1)}, u32[]{:S(2)}, u32[]{:S(2)}) async-start(bf16[8,128,256]{1,2,0:T(8,128)(2,1)} %copy.88), calls=%async_computation.3 | async-start | bytes 1048576 | tf_op jit(solution)/shard_map/all_to_all | solution.py:138
  201.2 13.0 %all-to-all-start.10 = ((f32[32,1,768]{2,1,0:T(1,128)}), f32[32,1,768]{2,1,0:T(1,128)S(1)}, u32[]{:S(2)}, u32[]{:S(2)}) async-start(f32[32,1,768]{2,1,0:T(1,128)} %all_to_all.107), calls=%async_computation.10 | async-start | bytes 196608 | tf_op jit(solution)/shard_map/all_to_all | solution.py:166
  (17 other events, 54.4 us)
Sparse Core Ops, SparseCore 0:
  10.6 84.6 all-gather.2

commit v2 on v0

v2 whole, which is shorter than its diff:
```python
import functools
import math

import jax
import jax.numpy as jnp
from jax import lax
from jax.experimental import pallas as pl
from jax.experimental.pallas import tpu as pltpu
from jax.sharding import PartitionSpec as P

MESH = pl.DeviceIdType.MESH
BF, F32 = jnp.bfloat16, jnp.float32
HD = 128
LANES = 128
EPS = 1e-06
Y = 4
CORES = 2
HALF = Y // CORES
LIVE, INV_HIGH, INV_LOW, TEXT_LEN = 64, 65, 66, 67


def mm(a, b):
    return jnp.dot(a, b, preferred_element_type=F32)


def mm_nt(a, b):
    return lax.dot_general(a, b, (((1,), (1,)), ((), ())), preferred_element_type=F32)


def mm_tn(a, b):
    return lax.dot_general(a, b, (((0,), (0,)), ((), ())), preferred_element_type=F32)


def iota(shape, dim):
    return lax.broadcasted_iota(jnp.int32, shape, dim)


def over(value, power):
    return lax.shift_right_logical(value, jnp.full_like(value, power.bit_length() - 1))


def within(value, power):
    return jnp.bitwise_and(value, power - 1)


def split(value):
    high = value.astype(BF)
    return high, (value - high.astype(F32)).astype(BF)


def kernel(
    n_dp,
    n_seq,
    text_len,
    codes,
    scales,
    slot_col,
    slot_row,
    embed,
    shift,
    scale,
    weight,
    text,
    grad_img,
    grad_txt,
    out_img,
    out_txt,
    code_out,
    embed_out,
    a_send,
    a_recv,
    own_tok,
    own_mods,
    tok,
    mods,
    wbuf,
    amat,
    mixed,
    const,
    qkv,
    dout,
    kaug,
    vaug,
    kt,
    vt,
    dot_t,
    valid_row,
    dk_acc,
    dv_acc,
    out_buf,
    dqkv,
    f_send,
    f_recv,
    back,
    g_send,
    g_recv,
    t_send,
    h1,
    h2,
    h3,
    send,
    recv,
    mod_send,
    ring_right,
    ring_left,
    ring_send,
):
    d, j = lax.axis_index("dp"), lax.axis_index("seq")
    z, y = lax.div(d, Y), lax.rem(d, Y)
    x, c = lax.div(j, CORES), lax.rem(j, CORES)
    slot, core = lax.rem(y, HALF), lax.div(y, HALF)
    own = core == c
    head = Y * x + y
    n_z, heads = n_dp // Y, Y * n_seq // CORES
    channels, width = embed.shape
    rows = weight.shape[0]
    local = grad_img.shape[0]
    tloc = grad_txt.shape[0]
    images, texts = local * n_seq, tloc * n_seq
    total = images + texts
    block = local // n_dp
    cols = 3 * HD

    def same(dp, seq):
        return jnp.logical_and(dp == d, seq == j)

    def remote(src, dst, k, dp, seq):
        pltpu.make_async_remote_copy(
            src_ref=src,
            dst_ref=dst,
            send_sem=send.at[k],
            recv_sem=recv.at[k],
            device_id=(dp, seq),
            device_id_type=MESH,
        ).start()

    def push(src, dst, k, dp, seq):
        @pl.when(same(dp, seq))
        def _():
            pltpu.make_async_copy(src, dst, recv.at[k]).start()

        @pl.when(jnp.logical_not(same(dp, seq)))
        def _():
            remote(src, dst, k, dp, seq)

    def arrived(ref, k):
        pltpu.make_async_copy(ref, ref, recv.at[k]).wait()

    def left_here(ref, k):
        pltpu.make_async_copy(ref, ref, send.at[k]).wait()

    def sent(some, whole, k):
        @pl.when(own)
        def _():
            left_here(some, k)

        @pl.when(jnp.logical_not(own))
        def _():
            left_here(whole, k)

    A, WY, MOD, TXT, DIMG, TOK, SIB, OIMG, OTXT, FEAT, G, H1, H2, H3, DTXT = range(15)

    def plane_peer(i):
        py = lax.rem(y + lax.div(i, n_seq), Y)
        return py, lax.rem(j + lax.rem(i, n_seq), n_seq)

    barrier = pltpu.get_barrier_semaphore()

    def greet_dp(i, carry):
        pl.semaphore_signal(
            barrier, inc=1, device_id=(lax.rem(d + i, n_dp), j), device_id_type=MESH
        )
        return carry

    lax.fori_loop(1, n_dp, greet_dp, 0)

    def greet_plane(i, carry):
        py = lax.rem(y + lax.div(i, n_seq - 1), Y)
        pj = lax.rem(j + 1 + lax.rem(i, n_seq - 1), n_seq)
        pl.semaphore_signal(barrier, inc=1, device_id=(z * Y + py, pj), device_id_type=MESH)
        return carry

    lax.fori_loop(0, Y * (n_seq - 1), greet_plane, 0)

    pick = (slot_col[...] == iota((n_dp, codes.shape[0]), 1)).astype(F32).astype(BF)
    used = jnp.sum(pick.astype(F32), axis=1, keepdims=True)
    pad_eye = (iota((channels, LANES), 0) == iota((channels, LANES), 1)).astype(F32).astype(BF)
    lane = iota((n_dp, LANES), 1)
    picked_scale = mm(mm(pick, scales[...]).astype(BF), pad_eye)
    picked_code = mm(pick, codes[...])
    tokens_of = []
    for t in range(block):
        part = picked_code[:, (t // 2) * LANES : (t // 2 + 1) * LANES]
        if t % 2:
            part = pltpu.roll(part, channels, 1)
        part = (part * picked_scale).astype(BF).astype(F32)
        tokens_of.append(jnp.where(lane == LIVE, used, part).astype(BF))
    stacked = jnp.concatenate(tokens_of, axis=0)
    shape = (8 * n_dp, local)
    r, k = iota(shape, 0), iota(shape, 1)
    spread = jnp.logical_and(over(r, 8) == within(k, n_dp), within(r, 8) == over(k, n_dp))
    a_send[...] = mm(spread.astype(F32).astype(BF), stacked)
    a_recv[pl.ds(pl.multiple_of(d * 8, 8), 8), :] = a_send[pl.ds(pl.multiple_of(d * 8, 8), 8), :]

    pl.semaphore_wait(barrier, n_dp - 1 + Y * (n_seq - 1))

    def tile(ref, i):
        return ref.at[pl.ds(pl.multiple_of(i * 8, 8), 8), :]

    def send_a(i, carry):
        p = lax.rem(d + i, n_dp)
        remote(tile(a_send, p), tile(a_recv, d), A, p, j)
        return carry

    lax.fori_loop(1, n_dp, send_a, 0)

    def wrows(first, count):
        return wbuf.at[pl.ds(pl.multiple_of(first * rows, 16), count * rows), :]

    for b in range(HALF):
        push(
            weight.at[:, pl.ds(b * cols, cols)],
            wrows(d, 1),
            WY,
            z * Y + HALF * c + b,
            CORES * x + core,
        )

    own_mods[0] = scale[...]
    own_mods[1] = shift[...]

    @pl.when(own)
    def _():
        for py in range(Y):

            @pl.when(py == y)
            def _():
                pltpu.make_async_copy(own_mods, mods.at[slot], recv.at[MOD]).start()

            @pl.when(py != y)
            def _():
                pltpu.make_async_remote_copy(
                    src_ref=own_mods,
                    dst_ref=mods.at[slot],
                    send_sem=mod_send.at[py],
                    recv_sem=recv.at[MOD],
                    device_id=(z * Y + py, j),
                    device_id_type=MESH,
                ).start()

    def lanes(i, count):
        return pl.ds(pl.multiple_of(i * count, LANES), count)

    def send_heads(i, carry):
        h = lax.rem(head + i, heads)
        dp, seq = z * Y + lax.rem(h, Y), CORES * lax.div(h, Y) + core
        push(
            text.at[:, lanes(h, cols)],
            qkv.at[slot, pl.ds(pl.multiple_of(j * tloc, 16), tloc), :],
            TXT,
            dp,
            seq,
        )
        push(
            grad_txt.at[:, lanes(h, HD)],
            dout.at[slot, pl.ds(pl.multiple_of(j * tloc, 16), tloc), :],
            DTXT,
            dp,
            seq,
        )
        push(
            grad_img.at[:, lanes(h, HD)],
            dout.at[slot, pl.ds(pl.multiple_of(texts + j * local, 16), local), :],
            DIMG,
            dp,
            seq,
        )
        return carry

    embed_f = embed[...].astype(F32)
    embed_centred = embed_f - jnp.sum(embed_f, axis=1, keepdims=True) * (1.0 / width)

    def shard(pz):
        return (pz * Y + c * HALF) * rows

    def wshard(pz, first=0, count=HALF * rows):
        return wbuf.at[pl.ds(pl.multiple_of(shard(pz) + first, 16), count), :]

    def hop(src_z, to, sems, step, first=0, count=HALF * rows):
        ref = wshard(src_z, first, count)
        pltpu.make_async_remote_copy(
            src_ref=ref,
            dst_ref=ref,
            send_sem=ring_send,
            recv_sem=sems.at[step],
            device_id=(to * Y + y, j),
            device_id_type=MESH,
        ).start()

    def landed(src_z, sems, step, first=0, count=HALF * rows):
        ref = wshard(src_z, first, count)
        pltpu.make_async_copy(ref, ref, sems.at[step]).wait()

    other = CORES * x + (1 - c)

    def to_sibling(src_z):
        ref = wshard(src_z)
        remote(ref, ref, SIB, d, other)

    up, down = lax.rem(z + 1, n_z), lax.rem(z + n_z - 1, n_z)
    last = n_z // 2 - 1
    piece = HALF * rows // 2
    arrived(wshard(z), WY)
    hop(z, up, ring_right, 0)
    hop(z, down, ring_left, 0)
    to_sibling(z)

    def ring_step(step):
        from_left = lax.rem(z + n_z - 1 - step, n_z)
        from_right = lax.rem(z + 1 + step, n_z)
        if step < last:
            landed(from_left, ring_right, step)
            if step + 1 < last:
                hop(from_left, up, ring_right, step + 1)
            else:
                hop(from_left, up, ring_right, step + 1, 0, piece)
            landed(from_right, ring_left, step)
            if step + 1 < last:
                hop(from_right, down, ring_left, step + 1)
            else:
                hop(from_right, down, ring_left, step + 1, piece, piece)
            to_sibling(from_left)
            to_sibling(from_right)
        else:
            landed(from_left, ring_right, step, 0, piece)
            landed(from_left, ring_left, step, piece, piece)
            to_sibling(from_left)

    lax.fori_loop(0, heads, send_heads, 0)

    arrived(a_recv.at[pl.ds(0, 8 * (n_dp - 1)), :], A)
    shape = (local, 8 * n_dp)
    r, k = iota(shape, 0), iota(shape, 1)
    gather = jnp.logical_and(over(r, block) == over(k, 8), within(r, block) == within(k, 8))
    mine = mm(gather.astype(F32).astype(BF), a_recv[...].astype(BF))
    xs = mm(mine[:, :channels].astype(BF), embed[...])
    centred = xs - jnp.sum(xs, axis=1, keepdims=True) * (1.0 / width)
    inv = lax.rsqrt(jnp.sum(centred * centred, axis=1, keepdims=True) * (1.0 / width) + EPS)
    xhat = (centred * inv).astype(BF)
    inv_high, inv_low = split(inv)
    lane = iota((local, LANES), 1)
    mine = jnp.where(lane == INV_HIGH, inv_high.astype(F32), mine)
    mine = jnp.where(lane == INV_LOW, inv_low.astype(F32), mine)
    mine = jnp.where(lane == TEXT_LEN, text_len[0].astype(F32), mine)
    own_tok[...] = mine.astype(BF)

    def send_tok(i, carry):
        h = lax.rem(head + i, heads)
        push(
            own_tok,
            tok.at[pl.ds(pl.multiple_of(slot * images + j * local, 16), local), :],
            TOK,
            z * Y + lax.rem(h, Y),
            CORES * lax.div(h, Y) + core,
        )
        return carry

    lax.fori_loop(0, heads, send_tok, 0)

    back[...] = jnp.zeros_like(back)
    back[:, :channels] = mm_nt(xhat, embed[...])

    arrived(mods, MOD)
    tail = jnp.zeros((16, width), F32)
    at = iota((16, width), 0)
    for u in range(HALF):
        high, low = split(embed_centred * (1.0 + mods[u, 0]))
        amat[u * channels : (u + 1) * channels, :] = high
        amat[(HALF + u) * channels : (HALF + u + 1) * channels, :] = low
        high, low = split(mods[u, 1])
        tail = jnp.where(at == u, high.astype(F32), tail)
        tail = jnp.where(at == HALF + u, low.astype(F32), tail)
    amat[2 * HALF * channels :, :] = tail.astype(BF)

    for step in range(last + 1):
        ring_step(step)

    arrived(wbuf.at[pl.ds(0, n_z * HALF * rows), :], SIB)
    product = mm(amat[...], wbuf[...])
    for u in range(HALF):
        mixed[u] = jnp.zeros_like(mixed[u])
        high, low = split(
            product[u * channels : (u + 1) * channels]
            + product[(HALF + u) * channels : (HALF + u + 1) * channels]
        )
        mixed[u, 0, :channels] = high
        mixed[u, 1, :channels] = low
        base = 2 * HALF * channels
        const[u] = product[base + u : base + u + 1] + product[base + HALF + u : base + HALF + u + 1]

    arrived(tok, TOK)
    arrived(qkv.at[:, pl.ds(0, texts), :], TXT)
    lane = iota((images, LANES), 1)
    tlane = iota((texts, LANES), 1)
    trow = iota((texts, LANES), 0)
    for u in range(HALF):
        tk = tok[u * images : (u + 1) * images]
        tf = tk.astype(F32)
        invs = tf[:, INV_HIGH : INV_HIGH + 1] + tf[:, INV_LOW : INV_LOW + 1]
        got = (mm(tk, mixed[u, 0]) + mm(tk, mixed[u, 1])) * invs + const[u]
        qkv[u, texts:, :] = got.astype(BF)
        length = tf[0:1, TEXT_LEN : TEXT_LEN + 1]
        kaug[u, :, :HD] = qkv[u, :, HD : 2 * HD]
        kaug[u, texts:, HD:] = jnp.where(lane == LIVE, (tf - 1.0) * 1e30, 0.0).astype(BF)
        bad = jnp.logical_and(tlane == LIVE, trow.astype(F32) >= length)
        kaug[u, :texts, HD:] = jnp.where(bad, -1e30, 0.0).astype(BF)
        vaug[u, :, :HD] = qkv[u, :, 2 * HD :]
        vaug[u, :, HD:] = jnp.ones((total, LANES), BF)
        kt[u] = qkv[u, :, HD : 2 * HD].T
        vt[u, :HD, :] = qkv[u, :, 2 * HD :].T
        vt[u, HD:, :] = jnp.ones((16, total), BF)
        pick_live = (iota((8, LANES), 1) == LIVE).astype(F32).astype(BF)
        valid_row[u, :, texts:] = mm_nt(pick_live, tk)[0:1]
        valid_row[u, :, :texts] = (iota((1, texts), 1).astype(F32) < length).astype(F32)
    arrived(dout.at[:, pl.ds(texts, images), :], DIMG)
    arrived(dout.at[:, pl.ds(0, texts), :], DTXT)
    for u in range(HALF):
        dot_t[u] = dout[u].T
    dk_acc[...] = jnp.zeros_like(dk_acc)
    dv_acc[...] = jnp.zeros_like(dv_acc)

    qb = total // 3 if total % (3 * LANES) == 0 else total
    factor = 1.0 / math.sqrt(HD)
    log2e = factor * math.log2(math.e)

    def attend(i, carry):
        first = pl.multiple_of(i * qb, LANES)
        at = pl.ds(first, qb)
        for u in range(HALF):
            query = qkv[u, at, :HD]
            ones = (iota((qb, LANES), 1) == LIVE).astype(F32).astype(BF)
            score = mm_nt(kaug[u], jnp.concatenate([query, ones], axis=1))
            top = jnp.max(score, axis=0, keepdims=True)
            expo = jnp.exp2((score - top) * log2e).astype(BF)
            got = mm(vt[u], expo)
            share = 1.0 / got[HD : HD + 1]
            valid = valid_row[u, :, at]
            out_t = (got[:HD] * (share * valid)).astype(BF)
            out_buf[u, at, :] = out_t.T
            up_t = dot_t[u, :, at].astype(F32) * valid
            delta = jnp.sum(up_t * out_t.astype(F32), axis=0, keepdims=True) * share
            scaled = (up_t * share).astype(BF)
            high, low = split(delta)
            at_row = iota((LANES, qb), 0)
            tail = jnp.where(at_row == 0, -high.astype(F32), 0.0)
            tail = jnp.where(at_row == 1, -low.astype(F32), tail).astype(BF)
            dprob = mm(vaug[u], jnp.concatenate([scaled, tail], axis=0))
            dscore = expo * dprob.astype(BF)
            dv_acc[u] += mm_nt(expo, scaled)
            dk_acc[u] += mm(dscore, query)
            dq = mm(kt[u], dscore) * factor
            dqkv[u, at, :HD] = dq.T.astype(BF)
        return carry

    lax.fori_loop(0, total // qb, attend, 0)

    for u in range(HALF):
        for s in range(n_seq):
            dp = z * Y + c * HALF + u
            push(
                out_buf.at[u, pl.ds(texts + s * local, local), :],
                out_img.at[:, lanes(head, HD)],
                OIMG,
                dp,
                s,
            )
            push(
                out_buf.at[u, pl.ds(s * tloc, tloc), :],
                out_txt.at[:, lanes(head, HD)],
                OTXT,
                dp,
                s,
            )

    gram = jnp.zeros((LANES, LANES), F32)
    seen = []
    for u in range(HALF):
        dqkv[u, :, HD : 2 * HD] = (dk_acc[u] * factor).astype(BF)
        dqkv[u, :, 2 * HD :] = dv_acc[u].astype(BF)
        grad = dqkv[u, texts:, :]
        part = mm_nt(grad, mixed[u, 0])
        for s in range(n_seq):
            slab = part[s * local : (s + 1) * local]
            packed = slab[: local // 2] + pltpu.roll(slab[local // 2 :], channels, 1)
            f_send[u * n_seq + s] = packed.astype(BF)
            push(f_send.at[u * n_seq + s], f_recv.at[head], FEAT, z * Y + c * HALF + u, s)
        tk = tok[u * images : (u + 1) * images]
        tf = tk.astype(F32)
        invs = tf[:, INV_HIGH : INV_HIGH + 1] + tf[:, INV_LOW : INV_LOW + 1]
        project = jnp.sum(tf * part, axis=1, keepdims=True) * (invs * (1.0 / width))
        scaled = tf * invs
        gram += mm_tn((scaled * (invs * project)).astype(BF), tk)
        seen.append(mm_tn(scaled.astype(BF), grad)[:channels])
    spread = mm_nt(jnp.concatenate(seen, axis=0).astype(BF), wbuf[...])
    weight_grad = spread[:channels] * (1.0 + mods[0, 0])
    for u in range(1, HALF):
        weight_grad += spread[u * channels : (u + 1) * channels] * (1.0 + mods[u, 0])
    weight_grad -= jnp.sum(weight_grad, axis=1, keepdims=True) * (1.0 / width)
    embed_f = embed[...].astype(F32)
    embed_centred = embed_f - jnp.sum(embed_f, axis=1, keepdims=True) * (1.0 / width)
    weight_grad -= mm(gram[:channels, :channels].astype(BF), embed_centred.astype(BF))
    t_send[...] = weight_grad.astype(BF)

    er, ec = channels // Y, width // n_seq

    def chunk(ref, py, pj):
        return ref.at[pl.ds(pl.multiple_of(py * er, 16), er), lanes(pj, ec)]

    me = y * n_seq + j
    plane = Y * n_seq

    def send_h1(i, carry):
        py, pj = plane_peer(i)
        remote(chunk(t_send, py, pj), h1.at[me], H1, z * Y + py, pj)
        return carry

    lax.fori_loop(1, plane, send_h1, 0)
    h1[me] = chunk(t_send, y, j)[...]

    arrived(f_recv, FEAT)
    half = local // 2
    packed = jnp.sum(f_recv[...].astype(F32), axis=0)
    lane = iota((half, LANES), 1)
    feat = jnp.concatenate(
        [
            jnp.where(lane < channels, packed, 0.0),
            jnp.where(lane < channels, pltpu.roll(packed, channels, 1), 0.0),
        ],
        axis=0,
    )
    mine = own_tok[...].astype(F32)
    inv = mine[:, INV_HIGH : INV_HIGH + 1] + mine[:, INV_LOW : INV_LOW + 1]
    project = jnp.sum(mine * feat, axis=1, keepdims=True) * (inv * (1.0 / width))
    ddeq = inv * (feat - back[...] * project)
    shape = (8 * n_dp, local)
    r, k = iota(shape, 0), iota(shape, 1)
    scatter = jnp.logical_and(over(k, block) == over(r, 8), within(k, block) == within(r, 8))
    g_send[...] = mm(scatter.astype(F32).astype(BF), ddeq.astype(BF))

    def send_g(i, carry):
        p = lax.rem(d + i, n_dp)
        remote(tile(g_send, p), tile(g_recv, d), G, p, j)
        return carry

    lax.fori_loop(1, n_dp, send_g, 0)
    tile(g_recv, d)[...] = tile(g_send, d)[...]

    arrived(h1.at[pl.ds(0, plane - 1)], H1)
    h2[z] = jnp.sum(h1[...].astype(F32), axis=0).astype(BF)

    def send_h2(i, carry):
        p = lax.rem(z + i, n_z)
        remote(h2.at[z], h2.at[z], H2, p * Y + y, j)
        return carry

    lax.fori_loop(1, n_z, send_h2, 0)

    arrived(g_recv.at[pl.ds(0, 8 * (n_dp - 1)), :], G)
    blocks = codes.shape[0]
    shape = (n_dp, 8 * n_dp)
    widen = (iota(shape, 0) == over(iota(shape, 1), 8)).astype(F32).astype(BF)
    chosen = (slot_row[...] == iota((blocks, n_dp), 0)).astype(F32).astype(BF)
    chosen = mm(chosen, widen)
    row = within(iota((blocks, 8 * n_dp), 1), 8)
    returned = g_recv[...].astype(BF)
    pad_scale = mm(scales[...], pad_eye)
    codes_of = [
        mm(jnp.where(row == t, chosen, 0.0).astype(BF), returned) * pad_scale for t in range(block)
    ]
    for t in range(0, block, 2):
        code_out[:, t // 2 * LANES : (t // 2 + 1) * LANES] = codes_of[t] + pltpu.roll(
            codes_of[t + 1], channels, 1
        )

    arrived(h2.at[pl.ds(0, n_z - 1)], H2)
    chunk(h3, y, j)[...] = jnp.sum(h2[...].astype(F32), axis=0).astype(BF)

    def send_h3(i, carry):
        py, pj = plane_peer(i)
        ref = chunk(h3, y, j)
        remote(ref, ref, H3, z * Y + py, pj)
        return carry

    lax.fori_loop(1, plane, send_h3, 0)

    left_here(a_send.at[pl.ds(0, 8 * (n_dp - 1)), :], A)
    sent(weight.at[:, pl.ds(0, (HALF - 1) * cols)], weight.at[:, pl.ds(0, HALF * cols)], WY)

    @pl.when(own)
    def _():
        for py in range(Y):

            @pl.when(py != y)
            def _():
                pltpu.make_async_copy(own_mods, own_mods, mod_send.at[py]).wait()

    few = heads - 1
    sent(text.at[:, pl.ds(0, few * cols)], text, TXT)
    sent(grad_txt.at[:, pl.ds(0, few * HD)], grad_txt, DTXT)
    sent(grad_img.at[:, pl.ds(0, few * HD)], grad_img, DIMG)
    sent(tok.at[pl.ds(0, few * local), :], tok, TOK)
    left_here(wbuf.at[pl.ds(0, n_z * HALF * rows), :], SIB)
    gone = wbuf.at[pl.ds(0, (n_z - 1) * HALF * rows), :]
    pltpu.make_async_copy(gone, gone, ring_send).wait()
    sent(out_img.at[:, pl.ds(0, few * HD)], out_img, OIMG)
    sent(out_txt.at[:, pl.ds(0, few * HD)], out_txt, OTXT)
    sent(f_send.at[pl.ds(0, few)], f_send, FEAT)
    left_here(g_send.at[pl.ds(0, 8 * (n_dp - 1)), :], G)
    left_here(h1.at[pl.ds(0, plane - 1)], H1)
    left_here(h2.at[pl.ds(0, n_z - 1)], H2)
    left_here(h1.at[pl.ds(0, plane - 1)], H3)

    arrived(h1.at[pl.ds(0, plane - 1)], H3)
    embed_out[...] = h3[...].astype(F32)
    arrived(out_img, OIMG)
    arrived(out_txt, OTXT)


def per_device(
    n_dp,
    n_seq,
    latent_codes,
    latent_scales,
    send_list,
    embed_weight,
    modulation_offset,
    mod_scale,
    qkv_weight,
    text_qkv,
    text_len,
    out_grad_img,
    out_grad_txt,
):
    codes, scales = latent_codes[0, 0], latent_scales[0, 0]
    slots = send_list[0, 0]
    channels, width = embed_weight.shape
    local, tloc = out_grad_img.shape[1], out_grad_txt.shape[1]
    images, texts = local * n_seq, tloc * n_seq
    total = images + texts
    heads = Y * n_seq // CORES
    cols = 3 * HD
    n_z = n_dp // Y
    er, ec = channels // Y, width // n_seq
    vmem, hbm = pl.BlockSpec(memory_space=pltpu.VMEM), pl.BlockSpec(memory_space=pl.ANY)
    smem = pl.BlockSpec(memory_space=pltpu.SMEM)
    block = codes.shape[1]
    scratch = [
        pltpu.VMEM((8 * n_dp, LANES), F32),
        pltpu.VMEM((8 * n_dp, LANES), F32),
        pltpu.VMEM((local, LANES), BF),
        pltpu.VMEM((2, 1, width), F32),
        pltpu.VMEM((HALF * images, LANES), BF),
        pltpu.VMEM((HALF, 2, 1, width), F32),
        pltpu.VMEM((width, cols), BF),
        pltpu.VMEM((2 * HALF * channels + 16, width), BF),
        pltpu.VMEM((HALF, 2, LANES, cols), BF),
        pltpu.VMEM((HALF, 1, cols), F32),
        pltpu.VMEM((HALF, total, cols), BF),
        pltpu.VMEM((HALF, total, HD), BF),
        pltpu.VMEM((HALF, total, 2 * HD), BF),
        pltpu.VMEM((HALF, total, 2 * HD), BF),
        pltpu.VMEM((HALF, HD, total), BF),
        pltpu.VMEM((HALF, HD + 16, total), BF),
        pltpu.VMEM((HALF, HD, total), BF),
        pltpu.VMEM((HALF, 1, total), F32),
        pltpu.VMEM((HALF, total, HD), F32),
        pltpu.VMEM((HALF, total, HD), F32),
        pltpu.VMEM((HALF, total, HD), BF),
        pltpu.VMEM((HALF, total, cols), BF),
        pltpu.VMEM((heads, local // 2, LANES), BF),
        pltpu.VMEM((heads, local // 2, LANES), BF),
        pltpu.VMEM((local, LANES), F32),
        pltpu.VMEM((8 * n_dp, LANES), F32),
        pltpu.VMEM((8 * n_dp, LANES), F32),
        pltpu.VMEM((channels, width), BF),
        pltpu.VMEM((Y * n_seq, er, ec), BF),
        pltpu.VMEM((n_z, er, ec), BF),
        pltpu.VMEM((channels, width), BF),
        pltpu.SemaphoreType.DMA((16,)),
        pltpu.SemaphoreType.DMA((16,)),
        pltpu.SemaphoreType.DMA((Y,)),
        pltpu.SemaphoreType.DMA((n_z // 2,)),
        pltpu.SemaphoreType.DMA((n_z // 2,)),
        pltpu.SemaphoreType.DMA,
    ]
    out = pl.pallas_call(
        functools.partial(kernel, n_dp, n_seq),
        out_shape=(
            jax.ShapeDtypeStruct((local, heads * HD), BF),
            jax.ShapeDtypeStruct((tloc, heads * HD), BF),
            jax.ShapeDtypeStruct((codes.shape[0], block), F32),
            jax.ShapeDtypeStruct((channels, width), F32),
        ),
        in_specs=[smem] + [vmem] * 7 + [hbm] * 4,
        out_specs=(hbm, hbm, vmem, vmem),
        scratch_shapes=scratch,
        compiler_params=pltpu.CompilerParams(
            collective_id=0, has_side_effects=True, vmem_limit_bytes=48 * 1024 * 1024
        ),
    )(
        text_len,
        codes,
        scales,
        slots[:, None],
        slots[None, :],
        embed_weight,
        modulation_offset,
        mod_scale,
        qkv_weight,
        text_qkv[0],
        out_grad_img[0],
        out_grad_txt[0],
    )
    img, txt, code, grad = out
    return img[None], txt[None], code[None, None], grad


def solution(mesh):
    return jax.shard_map(
        functools.partial(per_device, mesh.shape["dp"], mesh.shape["seq"]),
        mesh=mesh,
        in_specs=(
            P("dp", "seq", None, None),
            P("dp", "seq", None, None),
            P("dp", "seq", None),
            P(),
            P("dp", None),
            P("dp", None),
            P("dp", "seq"),
            P("dp", "seq", None),
            P("dp"),
            P("dp", "seq", None),
            P("dp", "seq", None),
        ),
        out_specs=(P("dp", "seq", None), P("dp", "seq", None), P("dp", "seq", None, None), P()),
        check_vma=False,
    )
```

time: 508 us -> 99 us (0.19)
  waiting for transfers between devices: 353 us -> 0 us
  Pallas kernels: 0 us -> 88.2 us
  starting transfers between devices: 49.6 us -> 0 us
  matrix products: 37.2 us -> 0 us
  other arithmetic: 14.7 us -> 0 us
  between operations: 15.5 us -> 1.35 us
  blocking collectives: 14.1 us -> 0 us
  local copies, waits for them, and re-layouts: 22 us -> 9.07 us
    psum x1 -> x0, waiting for transfers between devices: 232 us -> none  [per_device(): embed_grad = lax.psum(dweight, ('dp', 'seq'))]
    pallas_call x0 -> x1, Pallas kernels: none -> 88.2 us  [per_device(): pl.pallas_call(functools.partial(kernel, n_dp, n_seq), out_shape=(jax.Sha...]
    all_to_all x8 -> x0, starting transfers between devices: 49.5 us -> none  [the longest x1 12 us: per_device(): lax.all_to_all(out_scales, 'dp', split_axis=0, concat_axis=0, tiled=True)]
    all_gather x2 -> x0, waiting for transfers between devices: 49.4 us -> none  [the longest x1 46.3 us: per_device(): lax.all_gather(normalized_local_rows, 'seq', axis=0, tiled=True)]
    reduce_scatter x1 -> x0, waiting for transfers between devices: 37.9 us -> none  [per_device(): lax.psum_scatter(dnormed_part.astype(jnp.bfloat16), 'seq', scatter_dimens...]
    all_to_all x8 -> x0, waiting for transfers between devices: 33 us -> none  [the longest x1 7.72 us: per_device(): lax.all_to_all(out_codes, 'dp', split_axis=0, concat_axis=0, tiled=True)]
    dot_general x11 -> x0, matrix products: 27 us -> none  [the longest x1 9.51 us: per_device(): jnp.dot(normed_all, lax.all_gather(qkv_weight, 'dp', axis=0, tiled=True),...]
    unnamed x1 -> x0, blocking collectives: 14.1 us -> none
  transfers between devices with their start and end apart: 12 -> 0, of which waited for: 10 -> 0; matrix products, arithmetic and copies ran while one was open for 5% -> 0% of each run, Pallas kernels for 0% -> 0%
where the time goes in v2:
time: 99 us; the launch traced here: 98.7 us
  Pallas kernels  88.2 us (89%)
  local copies, waits for them, and re-layouts  9.07 us (9%)
  between operations  1.35 us (1%)
    pallas_call x1, Pallas kernels, per_device(): pl.pallas_call(functools.partial(kernel, n_dp, n_seq), out_shape=(jax.Sha...  88.2 us
    unnamed x24, local copies, waits for them, and re-layouts  8.98 us

profile of v2, /device:TPU:1, one launch (start us, length us, event | category | flops | bytes accessed | tf_op | source)
XLA Modules:
  0.0 98.7 jit_solution(8399509056125453990)
XLA Ops:
  0.6 0.0 copy-start.8
  1.3 0.0 copy-start.9
  1.3 0.0 copy-start.5
  1.3 0.0 copy-start.6
  1.3 0.6 copy-done.9
  2.0 0.1 copy.15.slot_col
  2.0 0.0 copy-done.8
  2.0 0.0 copy-done.5
  2.0 0.0 copy-done.6
  2.1 0.0 copy-start
  2.1 1.0 %copy-done = bf16[1,128,2048]{2,1,0:T(8,128)(2,1)S(1)} copy-done((bf16[1,128,2048]{2,1,0:T(8,128)(2,1)S(1)}, bf16[1,128,2048]{2,1,0:T(8,128)(2,1)}, u32[]{:S(2)}) %copy-start) | copy-done | bytes 524312
  3.1 0.0 copy-start.1
  3.1 1.0 %copy-done.1 = bf16[64,3072]{1,0:T(8,128)(2,1)S(1)} copy-done((bf16[64,3072]{1,0:T(8,128)(2,1)S(1)}, bf16[64,3072]{1,0:T(8,128)(2,1)}, u32[]{:S(2)}) %copy-start.1) | copy-done | bytes 393240
  4.1 0.0 copy-start.2
  4.1 0.9 copy-done.2
  5.0 0.0 copy-start.3
  5.0 0.9 copy-done.3
  5.9 0.8 copy-done.4
  6.8 0.7 copy-done.7
  7.5 88.2 %shard_map.138 = (bf16[128,2048]{1,0:T(8,128)(2,1)S(1)}, bf16[16,2048]{1,0:T(8,128)(2,1)S(1)}, f32[20,256]{1,0:T(8,128)S(1)}, f32[64,3072]{1,0:T(8,128)S(1)}) custom-call(s32[1]{0:T(128)S(6)} %copy.20.text_len, bf16[20,256]{1,0:T(8,128)(2,1)S(1)} %bitcast.16, bf16[20,64]{1,0:T(8,128)(2,1)S(1)} %bitcast.17, s32[32,1]{1,0:T(8,128)S(1)} %copy.15.slot_col, ...), custom_call_target="tpu_custom_call" | custom-call | tf_op jit(solution)/shard_map/pallas_call | solution.py:696
  95.7 0.6 copy.16
  96.4 0.8 copy.21
  97.1 0.6 copy.22
  97.8 0.9 copy.23
  (2 shorter events, 0.0 us)
Async XLA Ops:
  0.6 1.4 %copy-start.8 = (bf16[1,1,20,64]{3,2,1,0:T(8,128)(2,1)S(1)}, bf16[1,1,20,64]{3,2,1,0:T(8,128)(2,1)}, u32[]{:S(2)}) copy-start(bf16[1,1,20,64]{3,2,1,0:T(8,128)(2,1)} %param.12) | copy-start | bytes 7684
  1.3 0.7 copy-start.9
  1.3 0.7 copy-start.5
  1.3 0.7 copy-start.6
  2.1 1.0 %copy-start = (bf16[1,128,2048]{2,1,0:T(8,128)(2,1)S(1)}, bf16[1,128,2048]{2,1,0:T(8,128)(2,1)}, u32[]{:S(2)}) copy-start(bf16[1,128,2048]{2,1,0:T(8,128)(2,1)} %param.20) | copy-start | bytes 1572868
  3.1 1.0 %copy-start.1 = (bf16[64,3072]{1,0:T(8,128)(2,1)S(1)}, bf16[64,3072]{1,0:T(8,128)(2,1)}, u32[]{:S(2)}) copy-start(bf16[64,3072]{1,0:T(8,128)(2,1)} %embed.1) | copy-start | bytes 1179652
  4.1 0.9 copy-start.2
  5.0 0.9 copy-start.3
  5.9 0.8 copy-start.4
  6.8 0.7 copy-start.7

commit v3 on v2

v3 whole, which is shorter than its diff:
```python
import functools
import math

import jax
import jax.numpy as jnp
from jax import lax
from jax.experimental import pallas as pl
from jax.experimental.pallas import tpu as pltpu
from jax.sharding import PartitionSpec as P

MESH = pl.DeviceIdType.MESH
CUT = 99
BF, F32 = jnp.bfloat16, jnp.float32
HD = 128
LANES = 128
EPS = 1e-06
Y = 4
CORES = 2
HALF = Y // CORES
LIVE, INV_HIGH, INV_LOW, TEXT_LEN = 64, 65, 66, 67


def mm(a, b):
    return jnp.dot(a, b, preferred_element_type=F32)


def mm_nt(a, b):
    return lax.dot_general(a, b, (((1,), (1,)), ((), ())), preferred_element_type=F32)


def mm_tn(a, b):
    return lax.dot_general(a, b, (((0,), (0,)), ((), ())), preferred_element_type=F32)


def iota(shape, dim):
    return lax.broadcasted_iota(jnp.int32, shape, dim)


def over(value, power):
    return lax.shift_right_logical(value, jnp.full_like(value, power.bit_length() - 1))


def within(value, power):
    return jnp.bitwise_and(value, power - 1)


def query_block(total):
    return total // 3 if total % (3 * LANES) == 0 else total


def split(value):
    high = value.astype(BF)
    return high, (value - high.astype(F32)).astype(BF)


def kernel(
    n_dp,
    n_seq,
    text_len_hbm,
    codes_hbm,
    scales_hbm,
    slots_hbm,
    embed_hbm,
    shift_hbm,
    scale_hbm,
    weight,
    text,
    grad_img,
    grad_txt,
    out_img,
    out_txt,
    code_out,
    embed_out,
    text_len,
    codes,
    scales,
    slot_row,
    embed,
    a_send,
    a_recv,
    own_tok,
    own_pack,
    tokp,
    own_mods,
    tok,
    mods,
    wbuf,
    amat,
    mixed,
    qkv,
    dout,
    kaug,
    vaug,
    kt,
    vt,
    ebuf,
    sbuf,
    mixed_t,
    wbar,
    centred_b,
    valid_row,
    dk_acc,
    dv_acc,
    out_buf,
    img_recv,
    txt_recv,
    dqkv,
    f_send,
    f_recv,
    back,
    g_send,
    g_recv,
    t_send,
    h1,
    h2,
    h3,
    load,
    store,
    send,
    recv,
    mod_send,
    ring_right,
    ring_left,
    ring_send,
):
    d, j = lax.axis_index("dp"), lax.axis_index("seq")
    z, y = lax.div(d, Y), lax.rem(d, Y)
    x, c = lax.div(j, CORES), lax.rem(j, CORES)
    slot, core = lax.rem(y, HALF), lax.div(y, HALF)
    own = core == c
    head = Y * x + y
    n_z, heads = n_dp // Y, Y * n_seq // CORES
    channels, width = embed_hbm.shape
    rows = weight.shape[0]
    local = grad_img.shape[0]
    tloc = grad_txt.shape[0]
    images, texts = local * n_seq, tloc * n_seq
    total = images + texts
    block = local // n_dp
    cols = 3 * HD

    def same(dp, seq):
        return jnp.logical_and(dp == d, seq == j)

    def remote(src, dst, k, dp, seq):
        pltpu.make_async_remote_copy(
            src_ref=src,
            dst_ref=dst,
            send_sem=send.at[k],
            recv_sem=recv.at[k],
            device_id=(dp, seq),
            device_id_type=MESH,
        ).start()

    def push(src, dst, k, dp, seq):
        @pl.when(same(dp, seq))
        def _():
            pltpu.make_async_copy(src, dst, recv.at[k]).start()

        @pl.when(jnp.logical_not(same(dp, seq)))
        def _():
            remote(src, dst, k, dp, seq)

    def arrived(ref, k):
        pltpu.make_async_copy(ref, ref, recv.at[k]).wait()

    def left_here(ref, k):
        pltpu.make_async_copy(ref, ref, send.at[k]).wait()

    def sent(some, whole, k):
        @pl.when(own)
        def _():
            left_here(some, k)

        @pl.when(jnp.logical_not(own))
        def _():
            left_here(whole, k)

    A, MOD, TXT, DIMG, TOK, SIB, OIMG, OTXT, FEAT, G, H1, H2, H3, DTXT, WY = range(15)

    def plane_peer(i):
        py = lax.rem(y + lax.div(i, n_seq), Y)
        return py, lax.rem(j + lax.rem(i, n_seq), n_seq)

    loads = [
        pltpu.make_async_copy(src, dst, load.at[i])
        for i, (src, dst) in enumerate(
            (
                (slots_hbm, slot_row),
                (codes_hbm, codes),
                (scales_hbm, scales),
                (embed_hbm, embed),
                (scale_hbm, own_mods.at[0]),
                (shift_hbm, own_mods.at[1]),
                (text_len_hbm, text_len),
            )
        )
    ]
    for copy in loads:
        copy.start()

    barrier = pltpu.get_barrier_semaphore()

    def greet_dp(i, carry):
        pl.semaphore_signal(
            barrier, inc=1, device_id=(lax.rem(d + i, n_dp), j), device_id_type=MESH
        )
        return carry

    lax.fori_loop(1, n_dp, greet_dp, 0)

    def greet_plane(i, carry):
        py = lax.rem(y + lax.div(i, n_seq - 1), Y)
        pj = lax.rem(j + 1 + lax.rem(i, n_seq - 1), n_seq)
        pl.semaphore_signal(barrier, inc=1, device_id=(z * Y + py, pj), device_id_type=MESH)
        return carry

    lax.fori_loop(0, Y * (n_seq - 1), greet_plane, 0)

    for copy in loads[:3]:
        copy.wait()
    square = (n_dp, n_dp)
    diagonal = iota(square, 0) == iota(square, 1)
    slot_col = jnp.sum(
        jnp.where(diagonal, slot_row[...].astype(F32), 0.0), axis=1, keepdims=True
    ).astype(jnp.int32)
    pick = (slot_col == iota((n_dp, codes.shape[0]), 1)).astype(F32).astype(BF)
    used = jnp.sum(pick.astype(F32), axis=1, keepdims=True)
    pad_eye = (iota((channels, LANES), 0) == iota((channels, LANES), 1)).astype(F32).astype(BF)
    lane = iota((n_dp, LANES), 1)
    picked_scale = mm(mm(pick, scales[...]).astype(BF), pad_eye)
    picked_code = mm(pick, codes[...])
    for t in range(block):
        part = picked_code[:, (t // 2) * LANES : (t // 2 + 1) * LANES]
        if t % 2:
            part = pltpu.roll(part, channels, 1)
        part = (part * picked_scale).astype(BF).astype(F32)
        a_send[:, t, :] = jnp.where(lane == LIVE, used, part)
    a_recv[d] = a_send[d]

    pl.semaphore_wait(barrier, n_dp - 1 + Y * (n_seq - 1))

    def wrows(first, count):
        return wbuf.at[pl.ds(pl.multiple_of(first * rows, 16), count * rows), :]

    for b in range(HALF):
        push(
            weight.at[:, pl.ds(b * cols, cols)],
            wrows(d, 1),
            WY + slot,
            z * Y + HALF * c + b,
            CORES * x + core,
        )

    def send_a(i, carry):
        p = lax.rem(d + i, n_dp)
        remote(a_send.at[p], a_recv.at[d], A, p, j)
        return carry

    lax.fori_loop(1, n_dp, send_a, 0)

    for copy in loads[3:]:
        copy.wait()

    @pl.when(own)
    def _():
        for py in range(Y):

            @pl.when(py == y)
            def _():
                pltpu.make_async_copy(own_mods, mods.at[slot], recv.at[MOD]).start()

            @pl.when(py != y)
            def _():
                pltpu.make_async_remote_copy(
                    src_ref=own_mods,
                    dst_ref=mods.at[slot],
                    send_sem=mod_send.at[py],
                    recv_sem=recv.at[MOD],
                    device_id=(z * Y + py, j),
                    device_id_type=MESH,
                ).start()

    def lanes(i, count):
        return pl.ds(pl.multiple_of(i * count, LANES), count)

    def chip_of(i):
        h = lax.rem(head + i, heads)
        return h, z * Y + lax.rem(h, Y), CORES * lax.div(h, Y) + core

    def send_text(i, carry):
        h, dp, seq = chip_of(i)
        here = pl.ds(pl.multiple_of(j * tloc, 16), tloc)
        push(text.at[:, lanes(h, cols)], qkv.at[slot, here, :], TXT, dp, seq)
        return carry

    def send_grad(i, carry):
        h, dp, seq = chip_of(i)
        here = pl.ds(pl.multiple_of(j * tloc, 16), tloc)
        push(grad_txt.at[:, lanes(h, HD)], dout.at[slot, here, :], DTXT, dp, seq)
        here = pl.ds(pl.multiple_of(texts + j * local, 16), local)
        push(grad_img.at[:, lanes(h, HD)], dout.at[slot, here, :], DIMG, dp, seq)
        return carry

    embed_f = embed[...].astype(F32)
    embed_centred = embed_f - jnp.sum(embed_f, axis=1, keepdims=True) * (1.0 / width)

    def piece(pz, p):
        return wrows(pz * Y + c * HALF + p, 1)

    def hop(pz, p, to, sems, step):
        pltpu.make_async_remote_copy(
            src_ref=piece(pz, p),
            dst_ref=piece(pz, p),
            send_sem=ring_send,
            recv_sem=sems.at[step, p],
            device_id=(to * Y + y, j),
            device_id_type=MESH,
        ).start()

    def landed(pz, p, sems, step):
        pltpu.make_async_copy(piece(pz, p), piece(pz, p), sems.at[step, p]).wait()

    def to_sibling(pz, p):
        remote(piece(pz, p), piece(pz, p), SIB, d, CORES * x + (1 - c))

    up, down = lax.rem(z + 1, n_z), lax.rem(z + n_z - 1, n_z)
    last = n_z // 2 - 1
    for p in range(HALF):
        arrived(piece(z, p), WY + p)
        hop(z, p, up, ring_right, 0)
        hop(z, p, down, ring_left, 0)
        to_sibling(z, p)

    def ring_step(step):
        from_left = lax.rem(z + n_z - 1 - step, n_z)
        from_right = lax.rem(z + 1 + step, n_z)
        for p in range(HALF):
            if step < last:
                landed(from_left, p, ring_right, step)
                if step + 1 < last or p == 0:
                    hop(from_left, p, up, ring_right, step + 1)
                landed(from_right, p, ring_left, step)
                if step + 1 < last or p == 1:
                    hop(from_right, p, down, ring_left, step + 1)
                to_sibling(from_left, p)
                to_sibling(from_right, p)
            else:
                landed(from_left, p, (ring_right, ring_left)[p], step)
                to_sibling(from_left, p)

    lax.fori_loop(0, heads, send_text, 0)

    arrived(a_recv.at[pl.ds(0, n_dp - 1)], A)
    shape = (local, local)
    r, k = iota(shape, 0), iota(shape, 1)
    gather = jnp.logical_and(over(r, block) == within(k, n_dp), within(r, block) == over(k, n_dp))
    gather = gather.astype(F32).astype(BF)
    stacked = jnp.concatenate([a_recv[:, t, :] for t in range(block)], axis=0)
    mine = mm(gather, stacked.astype(BF))
    xs = mm(mine[:, :channels].astype(BF), embed[...])
    centred = xs - jnp.sum(xs, axis=1, keepdims=True) * (1.0 / width)
    inv = lax.rsqrt(jnp.sum(centred * centred, axis=1, keepdims=True) * (1.0 / width) + EPS)
    xhat = (centred * inv).astype(BF)
    inv_high, inv_low = split(inv)
    lane = iota((local, LANES), 1)
    mine = jnp.where(lane == INV_HIGH, inv_high.astype(F32), mine)
    mine = jnp.where(lane == INV_LOW, inv_low.astype(F32), mine)
    mine = jnp.where(lane == TEXT_LEN, text_len[0].astype(F32), mine)
    own_tok[...] = mine.astype(BF)
    half = local // 2
    only = jnp.where(lane < channels, mine, 0.0)
    own_pack[:half] = (only[:half] + pltpu.roll(only[half:], channels, 1)).astype(BF)
    flag = (iota((16, LANES), 1) == iota((16, LANES), 0) + LIVE).astype(F32).astype(BF)
    own_pack[half:] = jnp.zeros((16, LANES), BF)
    own_pack[half:, :local] = mm_nt(flag, own_tok[...]).astype(BF)

    def send_tok(i, carry):
        h, dp, seq = chip_of(i)
        push(own_pack, tokp.at[slot * n_seq + j], TOK, dp, seq)
        return carry

    lax.fori_loop(0, heads, send_tok, 0)
    ring_step(0)
    back[...] = jnp.zeros_like(back)
    back[:, :channels] = mm_nt(xhat, embed[...])

    arrived(mods, MOD)
    tail = jnp.zeros((16, width), F32)
    at = iota((16, width), 0)
    for u in range(HALF):
        high, low = split(embed_centred * (1.0 + mods[u, 0]))
        amat[u * channels : (u + 1) * channels, :] = high
        amat[(HALF + u) * channels : (HALF + u + 1) * channels, :] = low
        high, low = split(mods[u, 1])
        tail = jnp.where(at == u, high.astype(F32), tail)
        tail = jnp.where(at == HALF + u, low.astype(F32), tail)
        high, low = split((1.0 + mods[u, 0]) * (1.0 / width))
        tail = jnp.where(at == 2 * HALF + u, high.astype(F32), tail)
        tail = jnp.where(at == 3 * HALF + u, low.astype(F32), tail)
    amat[2 * HALF * channels :, :] = tail.astype(BF)
    centred_b[...] = embed_centred.astype(BF)

    for step in range(1, last):
        ring_step(step)

    arrived(tokp, TOK)
    half = local // 2
    low_lane = iota((half, LANES), 1) < channels
    for i in range(heads):
        packed = tokp[i, :half].astype(F32)
        flags = mm_tn(tokp[i, half:], flag)
        first = jnp.where(low_lane, packed, 0.0) + flags[:half]
        second = jnp.where(low_lane, pltpu.roll(packed, channels, 1), 0.0) + flags[half:local]
        tok[i * local : i * local + half] = first.astype(BF)
        tok[i * local + half : (i + 1) * local] = second.astype(BF)

    lane = iota((images, LANES), 1)
    tlane = iota((texts, LANES), 1)
    trow = iota((texts, LANES), 0)
    inv_rows = []
    for u in range(HALF):
        tk = tok[u * images : (u + 1) * images]
        tf = tk.astype(F32)
        length = tf[0:1, TEXT_LEN : TEXT_LEN + 1]
        kaug[u, texts:, HD:] = jnp.where(lane == LIVE, (tf - 1.0) * 1e30, 0.0).astype(BF)
        bad = jnp.logical_and(tlane == LIVE, trow.astype(F32) >= length)
        kaug[u, :texts, HD:] = jnp.where(bad, -1e30, 0.0).astype(BF)
        vaug[u, :, HD:] = jnp.ones((total, LANES), BF)
        vt[u, HD:, :] = jnp.ones((16, total), BF)
        flag_rows = mm_nt(flag, tk)
        inv_rows.append(flag_rows[1:2] + flag_rows[2:3])
        valid_row[u, :, texts:] = flag_rows[0:1]
        valid_row[u, :, :texts] = (iota((1, texts), 1).astype(F32) < length).astype(F32)
    dk_acc[...] = jnp.zeros_like(dk_acc)
    dv_acc[...] = jnp.zeros_like(dv_acc)
    arrived(qkv.at[:, pl.ds(0, texts), :], TXT)
    for u in range(HALF):
        kaug[u, :texts, :HD] = qkv[u, :texts, HD : 2 * HD]
        vaug[u, :texts, :HD] = qkv[u, :texts, 2 * HD :]
        kt[u, :, :texts] = qkv[u, :texts, HD : 2 * HD].T
        vt[u, :HD, :texts] = qkv[u, :texts, 2 * HD :].T

    lax.fori_loop(0, heads, send_grad, 0)
    ring_step(last)
    arrived(wbuf.at[pl.ds(0, n_z * HALF * rows), :], SIB)
    product = mm(amat[...], wbuf[...])
    base = 2 * HALF * channels
    for u in range(HALF):
        sums = (
            product[u * channels : (u + 1) * channels]
            + product[(HALF + u) * channels : (HALF + u + 1) * channels]
        )
        sums = jnp.concatenate([sums, jnp.zeros((LANES - channels, cols), F32)], axis=0)
        mixed[u, 0], mixed[u, 1] = split(sums)
        mixed_t[u, 0], mixed_t[u, 1] = split(sums.T)
        const = product[base + u : base + u + 1] + product[base + HALF + u : base + HALF + u + 1]
        wbar[u] = (
            product[base + 2 * HALF + u : base + 2 * HALF + u + 1]
            + product[base + 3 * HALF + u : base + 3 * HALF + u + 1]
        )
        const_t = jnp.broadcast_to(const[:, HD:], (LANES, 2 * HD)).T
        tk = tok[u * images : (u + 1) * images]
        tf = tk.astype(F32)
        invs = tf[:, INV_HIGH : INV_HIGH + 1] + tf[:, INV_LOW : INV_LOW + 1]
        got = ((mm(tk, mixed[u, 0]) + mm(tk, mixed[u, 1])) * invs + const).astype(BF)
        qkv[u, texts:, :HD] = got[:, :HD]
        kaug[u, texts:, :HD] = got[:, HD : 2 * HD]
        vaug[u, texts:, :HD] = got[:, 2 * HD :]
        got = mm_nt(mixed_t[u, 0, HD:], tk) + mm_nt(mixed_t[u, 1, HD:], tk)
        got = (got * inv_rows[u] + const_t[:, 0:1]).astype(BF)
        kt[u, :, texts:] = got[:HD]
        vt[u, :HD, texts:] = got[HD:]

    qb = query_block(total)
    factor = 1.0 / math.sqrt(HD)
    log2e = factor * math.log2(math.e)

    def attend(i, carry):
        first = pl.multiple_of(i * qb, LANES)
        at = pl.ds(first, qb)
        for u in range(HALF):
            query = qkv[u, at, :HD]
            ones = (iota((qb, LANES), 1) == LIVE).astype(F32).astype(BF)
            score = mm_nt(kaug[u], jnp.concatenate([query, ones], axis=1))
            top = jnp.max(score, axis=0, keepdims=True)
            expo = jnp.exp2((score - top) * log2e).astype(BF)
            got = mm(vt[u], expo)
            share = valid_row[u, :, at] / got[HD : HD + 1]
            out_buf[u, at, :] = (got[:HD] * share).T.astype(BF)
            sbuf[u, at, :] = jnp.broadcast_to(share, (LANES, qb)).T
            ebuf[u, i] = expo
        for u in range(HALF):
            dp = z * Y + c * HALF + u
            for s in range(n_seq):

                @pl.when(i == (texts + s * local) // qb)
                def _():
                    push(
                        out_buf.at[u, pl.ds(texts + s * local, local), :],
                        img_recv.at[:, lanes(head, HD)],
                        OIMG,
                        dp,
                        s,
                    )

                @pl.when(i == 0)
                def _():
                    push(
                        out_buf.at[u, pl.ds(s * tloc, tloc), :],
                        txt_recv.at[:, lanes(head, HD)],
                        OTXT,
                        dp,
                        s,
                    )

        return carry

    lax.fori_loop(0, total // qb, attend, 0)

    def attend_back(i, carry):
        at = pl.ds(pl.multiple_of(i * qb, LANES), qb)
        lane = iota((qb, LANES), 1)
        for u in range(HALF):
            expo = ebuf[u, i]
            share = sbuf[u, at, :]
            up = dout[u, at, :].astype(F32)
            delta = jnp.sum(up * out_buf[u, at, :].astype(F32), axis=1, keepdims=True) * share
            scaled = (up * share).astype(BF)
            high, low = split(delta)
            tail = jnp.where(lane == 0, -high.astype(F32), 0.0)
            tail = jnp.where(lane == 1, -low.astype(F32), tail).astype(BF)
            dprob = mm_nt(vaug[u], jnp.concatenate([scaled, tail], axis=1))
            dscore = expo * dprob.astype(BF)
            dv_acc[u] += mm(expo, scaled)
            dk_acc[u] += mm(dscore, qkv[u, at, :HD])
            dqkv[u, at, :HD] = (mm(kt[u], dscore) * factor).T.astype(BF)
        return carry

    arrived(dout.at[:, pl.ds(texts, images), :], DIMG)
    arrived(dout.at[:, pl.ds(0, texts), :], DTXT)
    lax.fori_loop(0, total // qb, attend_back, 0)

    gram = jnp.zeros((LANES, LANES), F32)
    seen = []
    for u in range(HALF):
        dqkv[u, :, HD : 2 * HD] = (dk_acc[u] * factor).astype(BF)
        dqkv[u, :, 2 * HD :] = dv_acc[u].astype(BF)
        grad = dqkv[u, texts:, :]
        part = mm(grad, mixed_t[u, 0])
        for s in range(n_seq):
            slab = part[s * local : (s + 1) * local]
            packed = slab[: local // 2] + pltpu.roll(slab[local // 2 :], channels, 1)
            f_send[u * n_seq + s] = packed.astype(BF)
            push(f_send.at[u * n_seq + s], f_recv.at[head], FEAT, z * Y + c * HALF + u, s)
        tk = tok[u * images : (u + 1) * images]
        tf = tk.astype(F32)
        invs = tf[:, INV_HIGH : INV_HIGH + 1] + tf[:, INV_LOW : INV_LOW + 1]
        project = jnp.sum(tf * part, axis=1, keepdims=True) * (invs * (1.0 / width))
        scaled = tf * invs
        gram += mm_tn((scaled * (invs * project)).astype(BF), tk)
        seen.append(mm_tn(scaled.astype(BF), grad)[:channels])
    seen = jnp.concatenate(seen, axis=0).astype(BF)
    gram = gram[:channels, :channels].astype(BF)
    average = jnp.zeros((channels, 1), F32)
    for u in range(HALF):
        mine = seen[u * channels : (u + 1) * channels].astype(F32)
        average += jnp.sum(mine * wbar[u], axis=1, keepdims=True)

    er, ec = channels // Y, width // n_seq

    def chunk(ref, py, pj):
        return ref.at[pl.ds(pl.multiple_of(py * er, 16), er), lanes(pj, ec)]

    me = y * n_seq + j
    plane = Y * n_seq

    def weight_block(i, carry):
        q = lax.rem(j + i, n_seq)
        at = lanes(q, ec)
        spread = mm_nt(seen, wbuf[pl.ds(pl.multiple_of(q * ec, LANES), ec), :])
        part = -mm(gram, centred_b[:, at]) - average
        for u in range(HALF):
            part += spread[u * channels : (u + 1) * channels] * (1.0 + mods[u, 0, :, at])
        t_send[:, at] = part.astype(BF)
        for py in range(Y):

            @pl.when(jnp.logical_not(jnp.logical_and(py == y, q == j)))
            def _():
                remote(chunk(t_send, py, q), h1.at[me], H1, z * Y + py, q)

        return carry

    lax.fori_loop(0, n_seq, weight_block, 0)
    h1[me] = chunk(t_send, y, j)[...]

    arrived(f_recv, FEAT)
    half = local // 2
    packed = jnp.sum(f_recv[...].astype(F32), axis=0)
    lane = iota((half, LANES), 1)
    feat = jnp.concatenate(
        [
            jnp.where(lane < channels, packed, 0.0),
            jnp.where(lane < channels, pltpu.roll(packed, channels, 1), 0.0),
        ],
        axis=0,
    )
    mine = own_tok[...].astype(F32)
    inv = mine[:, INV_HIGH : INV_HIGH + 1] + mine[:, INV_LOW : INV_LOW + 1]
    project = jnp.sum(mine * feat, axis=1, keepdims=True) * (inv * (1.0 / width))
    ddeq = inv * (feat - back[...] * project)
    spread = mm_tn(gather, ddeq.astype(BF))
    for t in range(block):
        g_send[:, t, :] = spread[t * n_dp : (t + 1) * n_dp]

    def send_g(i, carry):
        p = lax.rem(d + i, n_dp)
        remote(g_send.at[p], g_recv.at[d], G, p, j)
        return carry

    lax.fori_loop(1, n_dp, send_g, 0)
    g_recv[d] = g_send[d]

    arrived(h1.at[pl.ds(0, plane - 1)], H1)
    h2[z] = jnp.sum(h1[...].astype(F32), axis=0).astype(BF)

    def send_h2(i, carry):
        p = lax.rem(z + i, n_z)
        remote(h2.at[z], h2.at[z], H2, p * Y + y, j)
        return carry

    lax.fori_loop(1, n_z, send_h2, 0)

    arrived(h2.at[pl.ds(0, n_z - 1)], H2)
    chunk(h3, y, j)[...] = jnp.sum(h2[...].astype(F32), axis=0).astype(BF)

    def send_h3(i, carry):
        py, pj = plane_peer(i)
        ref = chunk(h3, y, j)
        remote(ref, ref, H3, z * Y + py, pj)
        return carry

    lax.fori_loop(1, plane, send_h3, 0)

    arrived(img_recv, OIMG)
    arrived(txt_recv, OTXT)
    stores = [
        pltpu.make_async_copy(img_recv, out_img, store.at[0]),
        pltpu.make_async_copy(txt_recv, out_txt, store.at[1]),
    ]
    for copy in stores:
        copy.start()

    arrived(g_recv.at[pl.ds(0, n_dp - 1)], G)
    blocks = codes.shape[0]
    chosen = (slot_row[...] == iota((blocks, n_dp), 0)).astype(F32).astype(BF)
    pad_scale = mm(scales[...], pad_eye)
    codes_of = [mm(chosen, g_recv[:, t, :].astype(BF)) * pad_scale for t in range(block)]
    for t in range(0, block, 2):
        code_out[:, 0, t // 2 * LANES : (t // 2 + 1) * LANES] = codes_of[t] + pltpu.roll(
            codes_of[t + 1], channels, 1
        )

    left_here(a_send.at[pl.ds(0, n_dp - 1)], A)
    sent(weight.at[:, pl.ds(0, (HALF - 1) * cols)], weight.at[:, pl.ds(0, HALF * cols)], WY + slot)

    @pl.when(own)
    def _():
        for py in range(Y):

            @pl.when(py != y)
            def _():
                pltpu.make_async_copy(own_mods, own_mods, mod_send.at[py]).wait()

    few = heads - 1
    sent(text.at[:, pl.ds(0, few * cols)], text, TXT)
    sent(grad_txt.at[:, pl.ds(0, few * HD)], grad_txt, DTXT)
    sent(grad_img.at[:, pl.ds(0, few * HD)], grad_img, DIMG)
    sent(tokp.at[pl.ds(0, few)], tokp, TOK)
    left_here(wbuf.at[pl.ds(0, n_z * HALF * rows), :], SIB)
    gone = wbuf.at[pl.ds(0, (n_z - 1) * HALF * rows), :]
    pltpu.make_async_copy(gone, gone, ring_send).wait()
    sent(img_recv.at[:, pl.ds(0, few * HD)], img_recv, OIMG)
    sent(txt_recv.at[:, pl.ds(0, few * HD)], txt_recv, OTXT)
    sent(f_send.at[pl.ds(0, few)], f_send, FEAT)
    left_here(g_send.at[pl.ds(0, n_dp - 1)], G)
    left_here(h1.at[pl.ds(0, plane - 1)], H1)
    left_here(h2.at[pl.ds(0, n_z - 1)], H2)
    left_here(h1.at[pl.ds(0, plane - 1)], H3)

    arrived(h1.at[pl.ds(0, plane - 1)], H3)
    to_hbm = pltpu.make_async_copy(h3, embed_out, store.at[2])
    to_hbm.start()
    to_hbm.wait()
    for copy in stores:
        copy.wait()


def finish(*refs):
    sources, results, held = refs[:4], refs[4:8], refs[8:12]
    wide, came, went = refs[12:]
    inward = [
        pltpu.make_async_copy(sources[i], held[i], came.at[i]) for i in (3, 0, 1, 2)
    ]
    for copy in inward:
        copy.start()
    inward[0].wait()
    wide[...] = held[3][...].astype(F32)
    last = pltpu.make_async_copy(wide, results[3], went.at[3])
    last.start()
    outward = [pltpu.make_async_copy(held[i], results[i], went.at[i]) for i in range(3)]
    for before, copy in zip(inward[1:], outward):
        before.wait()
        copy.start()
    for copy in outward:
        copy.wait()
    last.wait()


def per_device(
    n_dp,
    n_seq,
    latent_codes,
    latent_scales,
    send_list,
    embed_weight,
    modulation_offset,
    mod_scale,
    qkv_weight,
    text_qkv,
    text_len,
    out_grad_img,
    out_grad_txt,
):
    codes, scales = latent_codes[0, 0], latent_scales[0, 0]
    slots = send_list[0, 0]
    channels, width = embed_weight.shape
    local, tloc = out_grad_img.shape[1], out_grad_txt.shape[1]
    images, texts = local * n_seq, tloc * n_seq
    total = images + texts
    heads = Y * n_seq // CORES
    cols = 3 * HD
    n_z = n_dp // Y
    er, ec = channels // Y, width // n_seq
    qb = query_block(total)
    vmem, hbm = pl.BlockSpec(memory_space=pltpu.VMEM), pl.BlockSpec(memory_space=pltpu.HBM)
    block = codes.shape[1]
    scratch = [
        pltpu.SMEM((1,), jnp.int32),
        pltpu.VMEM(codes.shape, BF),
        pltpu.VMEM(scales.shape, BF),
        pltpu.VMEM((1, n_dp), jnp.int32),
        pltpu.VMEM((channels, width), BF),
        pltpu.VMEM((n_dp, 4, LANES), F32),
        pltpu.VMEM((n_dp, 4, LANES), F32),
        pltpu.VMEM((local, LANES), BF),
        pltpu.VMEM((local // 2 + 16, LANES), BF),
        pltpu.VMEM((heads, local // 2 + 16, LANES), BF),
        pltpu.VMEM((2, 1, width), F32),
        pltpu.VMEM((HALF * images, LANES), BF),
        pltpu.VMEM((HALF, 2, 1, width), F32),
        pltpu.VMEM((width, cols), BF),
        pltpu.VMEM((2 * HALF * channels + 16, width), BF),
        pltpu.VMEM((HALF, 2, LANES, cols), BF),
        pltpu.VMEM((HALF, total, cols), BF),
        pltpu.VMEM((HALF, total, HD), BF),
        pltpu.VMEM((HALF, total, 2 * HD), BF),
        pltpu.VMEM((HALF, total, 2 * HD), BF),
        pltpu.VMEM((HALF, HD, total), BF),
        pltpu.VMEM((HALF, HD + 16, total), BF),
        pltpu.VMEM((HALF, total // qb, total, qb), BF),
        pltpu.VMEM((HALF, total, LANES), F32),
        pltpu.VMEM((HALF, 2, cols, LANES), BF),
        pltpu.VMEM((HALF, 1, cols), F32),
        pltpu.VMEM((channels, width), BF),
        pltpu.VMEM((HALF, 1, total), F32),
        pltpu.VMEM((HALF, total, HD), F32),
        pltpu.VMEM((HALF, total, HD), F32),
        pltpu.VMEM((HALF, total, HD), BF),
        pltpu.VMEM((local, heads * HD), BF),
        pltpu.VMEM((tloc, heads * HD), BF),
        pltpu.VMEM((HALF, total, cols), BF),
        pltpu.VMEM((heads, local // 2, LANES), BF),
        pltpu.VMEM((heads, local // 2, LANES), BF),
        pltpu.VMEM((local, LANES), F32),
        pltpu.VMEM((n_dp, 4, LANES), F32),
        pltpu.VMEM((n_dp, 4, LANES), F32),
        pltpu.VMEM((channels, width), BF),
        pltpu.VMEM((Y * n_seq, er, ec), BF),
        pltpu.VMEM((n_z, er, ec), BF),
        pltpu.VMEM((channels, width), BF),
        pltpu.SemaphoreType.DMA((7,)),
        pltpu.SemaphoreType.DMA((3,)),
        pltpu.SemaphoreType.DMA((16,)),
        pltpu.SemaphoreType.DMA((16,)),
        pltpu.SemaphoreType.DMA((Y,)),
        pltpu.SemaphoreType.DMA((n_z // 2, HALF)),
        pltpu.SemaphoreType.DMA((n_z // 2, HALF)),
        pltpu.SemaphoreType.DMA,
    ]
    out = pl.pallas_call(
        functools.partial(kernel, n_dp, n_seq),
        out_shape=(
            jax.ShapeDtypeStruct((local, heads * HD), BF),
            jax.ShapeDtypeStruct((tloc, heads * HD), BF),
            jax.ShapeDtypeStruct((codes.shape[0], 1, block), F32),
            jax.ShapeDtypeStruct((channels, width), BF),
        ),
        in_specs=[hbm] * 11,
        out_specs=(hbm, hbm, vmem, hbm),
        scratch_shapes=scratch,
        compiler_params=pltpu.CompilerParams(
            collective_id=0, has_side_effects=True, vmem_limit_bytes=61 * 1024 * 1024
        ),
    )(
        text_len,
        codes,
        scales,
        slots[None, :],
        embed_weight,
        modulation_offset,
        mod_scale,
        qkv_weight,
        text_qkv[0],
        out_grad_img[0],
        out_grad_txt[0],
    )
    img, txt, code, grad = pl.pallas_call(
        finish,
        out_shape=tuple(
            jax.ShapeDtypeStruct(part.shape, kind) for part, kind in zip(out, (BF, BF, F32, F32))
        ),
        in_specs=[hbm] * 4,
        out_specs=(hbm,) * 4,
        scratch_shapes=[pltpu.VMEM(part.shape, part.dtype) for part in out]
        + [
            pltpu.VMEM((channels, width), F32),
            pltpu.SemaphoreType.DMA((4,)),
            pltpu.SemaphoreType.DMA((4,)),
        ],
        compiler_params=pltpu.CompilerParams(vmem_limit_bytes=61 * 1024 * 1024),
    )(*out)
    return img[None], txt[None], code[:, 0][None, None], grad


def solution(mesh):
    return jax.shard_map(
        functools.partial(per_device, mesh.shape["dp"], mesh.shape["seq"]),
        mesh=mesh,
        in_specs=(
            P("dp", "seq", None, None),
            P("dp", "seq", None, None),
            P("dp", "seq", None),
            P(),
            P("dp", None),
            P("dp", None),
            P("dp", "seq"),
            P("dp", "seq", None),
            P("dp"),
            P("dp", "seq", None),
            P("dp", "seq", None),
        ),
        out_specs=(P("dp", "seq", None), P("dp", "seq", None), P("dp", "seq", None, None), P()),
        check_vma=False,
    )
```

time: 99 us -> 81.8 us (0.83)
  local copies, waits for them, and re-layouts: 9.07 us -> 0 us
  Pallas kernels: 88.2 us -> 80.4 us
    pallas_call x1, Pallas kernels: 88.2 us -> 78.2 us  [per_device(): pl.pallas_call(functools.partial(kernel, n_dp, n_seq), out_shape=(jax.Sha...]
    unnamed x24 -> x0, local copies, waits for them, and re-layouts: 8.98 us -> none
    pallas_call x0 -> x1, Pallas kernels: none -> 2.18 us  [per_device(): pl.pallas_call(finish, out_shape=tuple((jax.ShapeDtypeStruct(part.shape,...]
where the time goes in v3:
time: 81.8 us; the launch traced here: 81.7 us
  Pallas kernels  80.4 us (98%)
  between operations  1.29 us (2%)
    pallas_call x1, Pallas kernels, per_device(): pl.pallas_call(functools.partial(kernel, n_dp, n_seq), out_shape=(jax.Sha...  78.2 us
    pallas_call x1, Pallas kernels, per_device(): pl.pallas_call(finish, out_shape=tuple((jax.ShapeDtypeStruct(part.shape,...  2.18 us

profile of v3, /device:TPU:1, one launch (start us, length us, event | category | flops | bytes accessed | tf_op | source)
XLA Modules:
  0.0 81.7 jit_solution(15141780195443712857)
XLA Ops:
  1.3 78.2 %shard_map.138 = (bf16[128,2048]{1,0:T(8,128)(2,1)}, bf16[16,2048]{1,0:T(8,128)(2,1)}, f32[20,1,256]{2,1,0:T(1,128)}, bf16[64,3072]{1,0:T(8,128)(2,1)}) custom-call(s32[1]{0:T(128)S(6)} %copy.16.text_len_hbm, bf16[20,256]{1,0:T(8,128)(2,1)} %bitcast.14, bf16[20,64]{1,0:T(8,128)(2,1)} %bitcast.15, s32[1,32]{1,0:T(1,128)} %bitcast.16, ...), custom_call_target="tpu_custom_call" | custom-call | tf_op jit(solution)/shard_map/pallas_call | solution.py:801
  79.5 2.2 %shard_map.139 = (bf16[128,2048]{1,0:T(8,128)(2,1)}, bf16[16,2048]{1,0:T(8,128)(2,1)}, f32[20,1,256]{2,1,0:T(1,128)}, f32[64,3072]{1,0:T(8,128)}) custom-call(bf16[128,2048]{1,0:T(8,128)(2,1)} %get-tuple-element.12.refs_0_, bf16[16,2048]{1,0:T(8,128)(2,1)} %get-tuple-element.13.refs_1_, f32[20,1,256]{2,1,0:T(1,128)} %get-tuple-element.14.refs_2_, ...), custom_call_target="tpu_custom_call" | custom-call | tf_op jit(solution)/shard_map/pallas_call | solution.py:828

commit v4 on v3

--- a/solution.py
+++ b/solution.py
@@ -42,10 +42,6 @@
 
 def within(value, power):
     return jnp.bitwise_and(value, power - 1)
-
-
-def query_block(total):
-    return total // 3 if total % (3 * LANES) == 0 else total
 
 
 def split(value):
@@ -98,9 +94,9 @@
     mixed_t,
     wbar,
     centred_b,
+    inv_row,
+    scaled_t,
     valid_row,
-    dk_acc,
-    dv_acc,
     out_buf,
     img_recv,
     txt_recv,
@@ -114,6 +110,7 @@
     h1,
     h2,
     h3,
+    whole,
     load,
     store,
     send,
@@ -161,6 +158,15 @@
         def _():
             remote(src, dst, k, dp, seq)
 
+    def each(send_one):
+        send_one(0, push)
+
+        def others(i, carry):
+            send_one(i, remote)
+            return carry
+
+        lax.fori_loop(1, heads, others, 0)
+
     def arrived(ref, k):
         pltpu.make_async_copy(ref, ref, recv.at[k]).wait()
 
@@ -179,7 +185,7 @@
     A, MOD, TXT, DIMG, TOK, SIB, OIMG, OTXT, FEAT, G, H1, H2, H3, DTXT, WY = range(15)
 
     def plane_peer(i):
-        py = lax.rem(y + lax.div(i, n_seq), Y)
+        py = lax.rem(y + lax.div(i, n_seq) + Y // 2, Y)
         return py, lax.rem(j + lax.rem(i, n_seq), n_seq)
 
     loads = [
@@ -288,19 +294,17 @@
         h = lax.rem(head + i, heads)
         return h, z * Y + lax.rem(h, Y), CORES * lax.div(h, Y) + core
 
-    def send_text(i, carry):
+    def send_text(i, how):
         h, dp, seq = chip_of(i)
         here = pl.ds(pl.multiple_of(j * tloc, 16), tloc)
-        push(text.at[:, lanes(h, cols)], qkv.at[slot, here, :], TXT, dp, seq)
-        return carry
-
-    def send_grad(i, carry):
+        how(text.at[:, lanes(h, cols)], qkv.at[slot, here, :], TXT, dp, seq)
+
+    def send_grad(i, how):
         h, dp, seq = chip_of(i)
         here = pl.ds(pl.multiple_of(j * tloc, 16), tloc)
-        push(grad_txt.at[:, lanes(h, HD)], dout.at[slot, here, :], DTXT, dp, seq)
+        how(grad_txt.at[:, lanes(h, HD)], dout.at[slot, here, :], DTXT, dp, seq)
         here = pl.ds(pl.multiple_of(texts + j * local, 16), local)
-        push(grad_img.at[:, lanes(h, HD)], dout.at[slot, here, :], DIMG, dp, seq)
-        return carry
+        how(grad_img.at[:, lanes(h, HD)], dout.at[slot, here, :], DIMG, dp, seq)
 
     embed_f = embed[...].astype(F32)
     embed_centred = embed_f - jnp.sum(embed_f, axis=1, keepdims=True) * (1.0 / width)
@@ -349,7 +353,7 @@
                 landed(from_left, p, (ring_right, ring_left)[p], step)
                 to_sibling(from_left, p)
 
-    lax.fori_loop(0, heads, send_text, 0)
+    each(send_text)
 
     arrived(a_recv.at[pl.ds(0, n_dp - 1)], A)
     shape = (local, local)
@@ -375,12 +379,11 @@
     own_pack[half:] = jnp.zeros((16, LANES), BF)
     own_pack[half:, :local] = mm_nt(flag, own_tok[...]).astype(BF)
 
-    def send_tok(i, carry):
+    def send_tok(i, how):
         h, dp, seq = chip_of(i)
-        push(own_pack, tokp.at[slot * n_seq + j], TOK, dp, seq)
-        return carry
-
-    lax.fori_loop(0, heads, send_tok, 0)
+        how(own_pack, tokp.at[slot * n_seq + j], TOK, dp, seq)
+
+    each(send_tok)
     ring_step(0)
     back[...] = jnp.zeros_like(back)
     back[:, :channels] = mm_nt(xhat, embed[...])
@@ -403,6 +406,7 @@
 
     for step in range(1, last):
         ring_step(step)
+    each(send_grad)
 
     arrived(tokp, TOK)
     half = local // 2
@@ -418,7 +422,6 @@
     lane = iota((images, LANES), 1)
     tlane = iota((texts, LANES), 1)
     trow = iota((texts, LANES), 0)
-    inv_rows = []
     for u in range(HALF):
         tk = tok[u * images : (u + 1) * images]
         tf = tk.astype(F32)
@@ -429,11 +432,10 @@
         vaug[u, :, HD:] = jnp.ones((total, LANES), BF)
         vt[u, HD:, :] = jnp.ones((16, total), BF)
         flag_rows = mm_nt(flag, tk)
-        inv_rows.append(flag_rows[1:2] + flag_rows[2:3])
+        inv_row[u] = flag_rows[1:2] + flag_rows[2:3]
+        scaled_t[u] = (tf.T * inv_row[u]).astype(BF)
         valid_row[u, :, texts:] = flag_rows[0:1]
         valid_row[u, :, :texts] = (iota((1, texts), 1).astype(F32) < length).astype(F32)
-    dk_acc[...] = jnp.zeros_like(dk_acc)
-    dv_acc[...] = jnp.zeros_like(dv_acc)
     arrived(qkv.at[:, pl.ds(0, texts), :], TXT)
     for u in range(HALF):
         kaug[u, :texts, :HD] = qkv[u, :texts, HD : 2 * HD]
@@ -441,7 +443,6 @@
         kt[u, :, :texts] = qkv[u, :texts, HD : 2 * HD].T
         vt[u, :HD, :texts] = qkv[u, :texts, 2 * HD :].T
 
-    lax.fori_loop(0, heads, send_grad, 0)
     ring_step(last)
     arrived(wbuf.at[pl.ds(0, n_z * HALF * rows), :], SIB)
     product = mm(amat[...], wbuf[...])
@@ -468,98 +469,65 @@
         kaug[u, texts:, :HD] = got[:, HD : 2 * HD]
         vaug[u, texts:, :HD] = got[:, 2 * HD :]
         got = mm_nt(mixed_t[u, 0, HD:], tk) + mm_nt(mixed_t[u, 1, HD:], tk)
-        got = (got * inv_rows[u] + const_t[:, 0:1]).astype(BF)
+        got = (got * inv_row[u] + const_t[:, 0:1]).astype(BF)
         kt[u, :, texts:] = got[:HD]
         vt[u, :HD, texts:] = got[HD:]
 
-    qb = query_block(total)
     factor = 1.0 / math.sqrt(HD)
     log2e = factor * math.log2(math.e)
 
-    def attend(i, carry):
-        first = pl.multiple_of(i * qb, LANES)
-        at = pl.ds(first, qb)
-        for u in range(HALF):
-            query = qkv[u, at, :HD]
-            ones = (iota((qb, LANES), 1) == LIVE).astype(F32).astype(BF)
-            score = mm_nt(kaug[u], jnp.concatenate([query, ones], axis=1))
-            top = jnp.max(score, axis=0, keepdims=True)
-            expo = jnp.exp2((score - top) * log2e).astype(BF)
-            got = mm(vt[u], expo)
-            share = valid_row[u, :, at] / got[HD : HD + 1]
-            out_buf[u, at, :] = (got[:HD] * share).T.astype(BF)
-            sbuf[u, at, :] = jnp.broadcast_to(share, (LANES, qb)).T
-            ebuf[u, i] = expo
-        for u in range(HALF):
-            dp = z * Y + c * HALF + u
-            for s in range(n_seq):
-
-                @pl.when(i == (texts + s * local) // qb)
-                def _():
-                    push(
-                        out_buf.at[u, pl.ds(texts + s * local, local), :],
-                        img_recv.at[:, lanes(head, HD)],
-                        OIMG,
-                        dp,
-                        s,
-                    )
-
-                @pl.when(i == 0)
-                def _():
-                    push(
-                        out_buf.at[u, pl.ds(s * tloc, tloc), :],
-                        txt_recv.at[:, lanes(head, HD)],
-                        OTXT,
-                        dp,
-                        s,
-                    )
-
-        return carry
-
-    lax.fori_loop(0, total // qb, attend, 0)
-
-    def attend_back(i, carry):
-        at = pl.ds(pl.multiple_of(i * qb, LANES), qb)
-        lane = iota((qb, LANES), 1)
-        for u in range(HALF):
-            expo = ebuf[u, i]
-            share = sbuf[u, at, :]
-            up = dout[u, at, :].astype(F32)
-            delta = jnp.sum(up * out_buf[u, at, :].astype(F32), axis=1, keepdims=True) * share
-            scaled = (up * share).astype(BF)
-            high, low = split(delta)
-            tail = jnp.where(lane == 0, -high.astype(F32), 0.0)
-            tail = jnp.where(lane == 1, -low.astype(F32), tail).astype(BF)
-            dprob = mm_nt(vaug[u], jnp.concatenate([scaled, tail], axis=1))
-            dscore = expo * dprob.astype(BF)
-            dv_acc[u] += mm(expo, scaled)
-            dk_acc[u] += mm(dscore, qkv[u, at, :HD])
-            dqkv[u, at, :HD] = (mm(kt[u], dscore) * factor).T.astype(BF)
-        return carry
+    for u in range(HALF):
+        query = qkv[u, :, :HD]
+        ones = (iota((total, LANES), 1) == LIVE).astype(F32).astype(BF)
+        score = mm_nt(kaug[u], jnp.concatenate([query, ones], axis=1))
+        top = jnp.max(score, axis=0, keepdims=True)
+        expo = jnp.exp2((score - top) * log2e).astype(BF)
+        got = mm(vt[u], expo)
+        share = valid_row[u] / got[HD : HD + 1]
+        out_buf[u] = (got[:HD] * share).T.astype(BF)
+        sbuf[u] = jnp.broadcast_to(share, (LANES, total)).T
+        ebuf[u] = expo
+
+    def slab(i):
+        u = lax.rem(slot + lax.div(i, n_seq), HALF)
+        return u, lax.rem(j + lax.rem(i, n_seq), n_seq)
+
+    def send_out(i, how):
+        u, s = slab(i)
+        dp = z * Y + c * HALF + u
+        rows_of = pl.ds(pl.multiple_of(texts + s * local, 16), local)
+        how(out_buf.at[u, rows_of, :], img_recv.at[:, lanes(head, HD)], OIMG, dp, s)
+        rows_of = pl.ds(pl.multiple_of(s * tloc, 16), tloc)
+        how(out_buf.at[u, rows_of, :], txt_recv.at[:, lanes(head, HD)], OTXT, dp, s)
+
+    each(send_out)
 
     arrived(dout.at[:, pl.ds(texts, images), :], DIMG)
     arrived(dout.at[:, pl.ds(0, texts), :], DTXT)
-    lax.fori_loop(0, total // qb, attend_back, 0)
+    lane = iota((total, LANES), 1)
+    for u in range(HALF):
+        expo, share = ebuf[u], sbuf[u]
+        up = dout[u].astype(F32)
+        delta = jnp.sum(up * out_buf[u].astype(F32), axis=1, keepdims=True) * share
+        scaled = (up * share).astype(BF)
+        high, low = split(delta)
+        tail = jnp.where(lane == 0, -high.astype(F32), 0.0)
+        tail = jnp.where(lane == 1, -low.astype(F32), tail).astype(BF)
+        dprob = mm_nt(vaug[u], jnp.concatenate([scaled, tail], axis=1))
+        dscore = expo * dprob.astype(BF)
+        dqkv[u, :, 2 * HD :] = mm(expo, scaled).astype(BF)
+        dqkv[u, :, HD : 2 * HD] = (mm(dscore, qkv[u, :, :HD]) * factor).astype(BF)
+        dqkv[u, :, :HD] = (mm(kt[u], dscore) * factor).T.astype(BF)
 
     gram = jnp.zeros((LANES, LANES), F32)
     seen = []
     for u in range(HALF):
-        dqkv[u, :, HD : 2 * HD] = (dk_acc[u] * factor).astype(BF)
-        dqkv[u, :, 2 * HD :] = dv_acc[u].astype(BF)
         grad = dqkv[u, texts:, :]
-        part = mm(grad, mixed_t[u, 0])
-        for s in range(n_seq):
-            slab = part[s * local : (s + 1) * local]
-            packed = slab[: local // 2] + pltpu.roll(slab[local // 2 :], channels, 1)
-            f_send[u * n_seq + s] = packed.astype(BF)
-            push(f_send.at[u * n_seq + s], f_recv.at[head], FEAT, z * Y + c * HALF + u, s)
-        tk = tok[u * images : (u + 1) * images]
-        tf = tk.astype(F32)
-        invs = tf[:, INV_HIGH : INV_HIGH + 1] + tf[:, INV_LOW : INV_LOW + 1]
-        project = jnp.sum(tf * part, axis=1, keepdims=True) * (invs * (1.0 / width))
-        scaled = tf * invs
-        gram += mm_tn((scaled * (invs * project)).astype(BF), tk)
-        seen.append(mm_tn(scaled.astype(BF), grad)[:channels])
+        seen.append(mm(scaled_t[u], grad)[:channels])
+        scaled = scaled_t[u].astype(F32)
+        project = jnp.sum(scaled * mm_nt(mixed[u, 0], grad), axis=0, keepdims=True)
+        project = project * (inv_row[u] * (1.0 / width))
+        gram += mm((scaled * project).astype(BF), tok[u * images : (u + 1) * images])
     seen = jnp.concatenate(seen, axis=0).astype(BF)
     gram = gram[:channels, :channels].astype(BF)
     average = jnp.zeros((channels, 1), F32)
@@ -568,9 +536,6 @@
         average += jnp.sum(mine * wbar[u], axis=1, keepdims=True)
 
     er, ec = channels // Y, width // n_seq
-
-    def chunk(ref, py, pj):
-        return ref.at[pl.ds(pl.multiple_of(py * er, 16), er), lanes(pj, ec)]
 
     me = y * n_seq + j
     plane = Y * n_seq
@@ -582,18 +547,40 @@
         part = -mm(gram, centred_b[:, at]) - average
         for u in range(HALF):
             part += spread[u * channels : (u + 1) * channels] * (1.0 + mods[u, 0, :, at])
-        t_send[:, at] = part.astype(BF)
         for py in range(Y):
+            t_send[py * n_seq + q] = part[py * er : (py + 1) * er].astype(BF)
 
             @pl.when(jnp.logical_not(jnp.logical_and(py == y, q == j)))
             def _():
-                remote(chunk(t_send, py, q), h1.at[me], H1, z * Y + py, q)
+                remote(t_send.at[py * n_seq + q], h1.at[me], H1, z * Y + py, q)
 
         return carry
 
     lax.fori_loop(0, n_seq, weight_block, 0)
-    h1[me] = chunk(t_send, y, j)[...]
-
+    h1[me] = t_send[me]
+
+    for u in range(HALF):
+        part = mm(dqkv[u, texts:, :], mixed_t[u, 0])
+        for s in range(n_seq):
+            own_part = part[s * local : (s + 1) * local]
+            packed = own_part[: local // 2] + pltpu.roll(own_part[local // 2 :], channels, 1)
+            f_send[u * n_seq + s] = packed.astype(BF)
+
+    def send_feat(i, how):
+        u, s = slab(i)
+        how(f_send.at[u * n_seq + s], f_recv.at[head], FEAT, z * Y + c * HALF + u, s)
+
+    each(send_feat)
+
+    arrived(h1.at[pl.ds(0, plane - 1)], H1)
+    h2[z] = jnp.sum(h1[...].astype(F32), axis=0).astype(BF)
+
+    def send_h2(i, carry):
+        p = lax.rem(z + i, n_z)
+        remote(h2.at[z], h2.at[z], H2, p * Y + y, j)
+        return carry
+
+    lax.fori_loop(1, n_z, send_h2, 0)
     arrived(f_recv, FEAT)
     half = local // 2
     packed = jnp.sum(f_recv[...].astype(F32), axis=0)
@@ -621,26 +608,19 @@
     lax.fori_loop(1, n_dp, send_g, 0)
     g_recv[d] = g_send[d]
 
-    arrived(h1.at[pl.ds(0, plane - 1)], H1)
-    h2[z] = jnp.sum(h1[...].astype(F32), axis=0).astype(BF)
-
-    def send_h2(i, carry):
-        p = lax.rem(z + i, n_z)
-        remote(h2.at[z], h2.at[z], H2, p * Y + y, j)
-        return carry
-
-    lax.fori_loop(1, n_z, send_h2, 0)
-
     arrived(h2.at[pl.ds(0, n_z - 1)], H2)
-    chunk(h3, y, j)[...] = jnp.sum(h2[...].astype(F32), axis=0).astype(BF)
+    h3[me] = jnp.sum(h2[...].astype(F32), axis=0).astype(BF)
 
     def send_h3(i, carry):
         py, pj = plane_peer(i)
-        ref = chunk(h3, y, j)
-        remote(ref, ref, H3, z * Y + py, pj)
+
+        @pl.when(i != Y // 2 * n_seq)
+        def _():
+            remote(h3.at[me], h3.at[me], H3, z * Y + py, pj)
+
         return carry
 
-    lax.fori_loop(1, plane, send_h3, 0)
+    lax.fori_loop(0, plane, send_h3, 0)
 
     arrived(img_recv, OIMG)
     arrived(txt_recv, OTXT)
@@ -689,7 +669,10 @@
     left_here(h1.at[pl.ds(0, plane - 1)], H3)
 
     arrived(h1.at[pl.ds(0, plane - 1)], H3)
-    to_hbm = pltpu.make_async_copy(h3, embed_out, store.at[2])
+    for py in range(Y):
+        for q in range(n_seq):
+            whole[py * er : (py + 1) * er, q * ec : (q + 1) * ec] = h3[py * n_seq + q]
+    to_hbm = pltpu.make_async_copy(whole, embed_out, store.at[2])
     to_hbm.start()
     to_hbm.wait()
     for copy in stores:
@@ -742,7 +725,6 @@
     cols = 3 * HD
     n_z = n_dp // Y
     er, ec = channels // Y, width // n_seq
-    qb = query_block(total)
     vmem, hbm = pl.BlockSpec(memory_space=pltpu.VMEM), pl.BlockSpec(memory_space=pltpu.HBM)
     block = codes.shape[1]
     scratch = [
@@ -768,14 +750,14 @@
         pltpu.VMEM((HALF, total, 2 * HD), BF),
         pltpu.VMEM((HALF, HD, total), BF),
         pltpu.VMEM((HALF, HD + 16, total), BF),
-        pltpu.VMEM((HALF, total // qb, total, qb), BF),
+        pltpu.VMEM((HALF, total, total), BF),
         pltpu.VMEM((HALF, total, LANES), F32),
         pltpu.VMEM((HALF, 2, cols, LANES), BF),
         pltpu.VMEM((HALF, 1, cols), F32),
         pltpu.VMEM((channels, width), BF),
+        pltpu.VMEM((HALF, 1, images), F32),
+        pltpu.VMEM((HALF, LANES, images), BF),
         pltpu.VMEM((HALF, 1, total), F32),
-        pltpu.VMEM((HALF, total, HD), F32),
-        pltpu.VMEM((HALF, total, HD), F32),
         pltpu.VMEM((HALF, total, HD), BF),
         pltpu.VMEM((local, heads * HD), BF),
         pltpu.VMEM((tloc, heads * HD), BF),
@@ -785,9 +767,10 @@
         pltpu.VMEM((local, LANES), F32),
         pltpu.VMEM((n_dp, 4, LANES), F32),
         pltpu.VMEM((n_dp, 4, LANES), F32),
-        pltpu.VMEM((channels, width), BF),
+        pltpu.VMEM((Y * n_seq, er, ec), BF),
         pltpu.VMEM((Y * n_seq, er, ec), BF),
         pltpu.VMEM((n_z, er, ec), BF),
+        pltpu.VMEM((Y * n_seq, er, ec), BF),
         pltpu.VMEM((channels, width), BF),
         pltpu.SemaphoreType.DMA((7,)),
         pltpu.SemaphoreType.DMA((3,)),

time: 81.8 us -> 75.9 us (0.928)
  Pallas kernels: 80.4 us -> 74.3 us
    pallas_call x1, Pallas kernels: 78.2 us -> 72.1 us  [per_device(): pl.pallas_call(functools.partial(kernel, n_dp, n_seq), out_shape=(jax.Sha...]
where the time goes in v4:
time: 75.9 us; the launch traced here: 75.8 us
  Pallas kernels  74.3 us (98%)
  between operations  1.45 us (2%)
    pallas_call x1, Pallas kernels, per_device(): pl.pallas_call(functools.partial(kernel, n_dp, n_seq), out_shape=(jax.Sha...  72.1 us
    pallas_call x1, Pallas kernels, per_device(): pl.pallas_call(finish, out_shape=tuple((jax.ShapeDtypeStruct(part.shape,...  2.18 us

profile of v4, /device:TPU:1, one launch (start us, length us, event | category | flops | bytes accessed | tf_op | source)
XLA Modules:
  0.0 75.8 jit_solution(4522334202840985368)
XLA Ops:
  1.3 72.1 %shard_map.138 = (bf16[128,2048]{1,0:T(8,128)(2,1)}, bf16[16,2048]{1,0:T(8,128)(2,1)}, f32[20,1,256]{2,1,0:T(1,128)}, bf16[64,3072]{1,0:T(8,128)(2,1)}) custom-call(s32[1]{0:T(128)S(6)} %copy.16.text_len_hbm, bf16[20,256]{1,0:T(8,128)(2,1)} %bitcast.14, bf16[20,64]{1,0:T(8,128)(2,1)} %bitcast.15, s32[1,32]{1,0:T(1,128)} %bitcast.16, ...), custom_call_target="tpu_custom_call" | custom-call | tf_op jit(solution)/shard_map/pallas_call | solution.py:784
  73.4 2.2 %shard_map.139 = (bf16[128,2048]{1,0:T(8,128)(2,1)}, bf16[16,2048]{1,0:T(8,128)(2,1)}, f32[20,1,256]{2,1,0:T(1,128)}, f32[64,3072]{1,0:T(8,128)}) custom-call(bf16[128,2048]{1,0:T(8,128)(2,1)} %get-tuple-element.12.refs_0_, bf16[16,2048]{1,0:T(8,128)(2,1)} %get-tuple-element.13.refs_1_, f32[20,1,256]{2,1,0:T(1,128)} %get-tuple-element.14.refs_2_, ...), custom_call_target="tpu_custom_call" | custom-call | tf_op jit(solution)/shard_map/pallas_call | solution.py:811

commit v5 on v4

--- a/solution.py
+++ b/solution.py
@@ -353,7 +353,6 @@
                 landed(from_left, p, (ring_right, ring_left)[p], step)
                 to_sibling(from_left, p)
 
-    each(send_text)
 
     arrived(a_recv.at[pl.ds(0, n_dp - 1)], A)
     shape = (local, local)
@@ -385,6 +384,7 @@
 
     each(send_tok)
     ring_step(0)
+    each(send_text)
     back[...] = jnp.zeros_like(back)
     back[:, :channels] = mm_nt(xhat, embed[...])
 

time: 75.9 us -> 76.4 us (level)
  no operation moved by 1% of the time
where the time goes in v5:
time: 76.4 us; the launch traced here: 76.3 us
  Pallas kernels  74.8 us (98%)
  between operations  1.45 us (2%)
    pallas_call x1, Pallas kernels, per_device(): pl.pallas_call(functools.partial(kernel, n_dp, n_seq), out_shape=(jax.Sha...  72.6 us
    pallas_call x1, Pallas kernels, per_device(): pl.pallas_call(finish, out_shape=tuple((jax.ShapeDtypeStruct(part.shape,...  2.18 us

profile of v5, /device:TPU:1, one launch (start us, length us, event | category | flops | bytes accessed | tf_op | source)
XLA Modules:
  0.0 76.3 jit_solution(3815952873998494395)
XLA Ops:
  1.3 72.6 %shard_map.138 = (bf16[128,2048]{1,0:T(8,128)(2,1)}, bf16[16,2048]{1,0:T(8,128)(2,1)}, f32[20,1,256]{2,1,0:T(1,128)}, bf16[64,3072]{1,0:T(8,128)(2,1)}) custom-call(s32[1]{0:T(128)S(6)} %copy.16.text_len_hbm, bf16[20,256]{1,0:T(8,128)(2,1)} %bitcast.14, bf16[20,64]{1,0:T(8,128)(2,1)} %bitcast.15, s32[1,32]{1,0:T(1,128)} %bitcast.16, ...), custom_call_target="tpu_custom_call" | custom-call | tf_op jit(solution)/shard_map/pallas_call | solution.py:784
  73.9 2.2 %shard_map.139 = (bf16[128,2048]{1,0:T(8,128)(2,1)}, bf16[16,2048]{1,0:T(8,128)(2,1)}, f32[20,1,256]{2,1,0:T(1,128)}, f32[64,3072]{1,0:T(8,128)}) custom-call(bf16[128,2048]{1,0:T(8,128)(2,1)} %get-tuple-element.12.refs_0_, bf16[16,2048]{1,0:T(8,128)(2,1)} %get-tuple-element.13.refs_1_, f32[20,1,256]{2,1,0:T(1,128)} %get-tuple-element.14.refs_2_, ...), custom_call_target="tpu_custom_call" | custom-call | tf_op jit(solution)/shard_map/pallas_call | solution.py:811
